TPU v7x, 512 devices: a whole 4x4x16 slice. The times are simulated.
512 devices in a mesh: group: 32 (over z_hi, y, core), head: 16 (over x, z_lo).
Axes of the slice: x: 4, y: 4, z: 16 (z_hi: 4, z_lo: 4; z = z_hi * 4 + z_lo), core: 2. Of those that a mesh axis runs over, the one named last changes fastest.
Arguments:
- queries: bfloat16 [1024, 4, 128, 576], P('group', None, 'head'), may hold values from -48 to 48
- new_latent: bfloat16 [1024, 4, 576], P('group'), may hold values from -4 to 4
- own_cache: bfloat16 [1024, 32, 576], P('group'), may hold values from -4 to 4
- prompt_pool: bfloat16 [32, 32, 64, 576], P('group', 'head'), may hold values from -4 to 4
- uv_weight: bfloat16 [128, 512, 128], P('head'), may hold values from -0.25 to 0.25
- owner: int32 [32], replicated, may hold values from 0 to 31, as said below
- route: int32 [32], P('group'), may hold values from 0 to 1
- prompt_len: int32 [1024], P('group'), may hold values from 1 to 2048, as said below
- page_table: int32 [32], replicated, may hold values from 0 to 31, each once
Outputs:
- attended: bfloat16 [1024, 4, 16384], P('group', None, 'head')
Inputs may be any that keep to these rules, and one draw needn't show every extreme that they name: `owner`: each of the 32 numbers appears once. `prompt_len`: the first request of every group reads the whole prompt. `page_table`: each of the 32 slots appears once.
All inputs are finite; a program needn't handle non-finite values.
Results may differ from a plain program's by a relative error of at most 0.0065.
Values may be sent and summed in bfloat16 or wider, within the bound.
No kernel may reach another device: no remote copies, remote signals or barrier semaphores. Data moves between devices by JAX's collectives and lax.ppermute only.
A program may use at most 64 MiB of HBM per device.

v0:
```python
import jax
import jax.numpy as jnp
from jax import lax
from jax.sharding import PartitionSpec as P

softmax_scale = 192.0 ** (-0.5)
lowest_score = -1e30


def from_root(value, axis, root):
    mine = lax.axis_index(axis) == root
    return lax.psum(jnp.where(mine, value, jnp.zeros_like(value)), axis)


def combine_stats(first, second):
    maxima = jnp.maximum(first[0], second[0])
    factor_one = jnp.exp(first[0] - maxima)
    factor_two = jnp.exp(second[0] - maxima)
    sums = first[1] * factor_one + second[1] * factor_two
    weighted = first[2] * factor_one[:, None] + second[2] * factor_two[:, None]
    return (maxima, sums, weighted)


def block_stats(query_rows, key_rows, visible, rank_dim):
    key_count = key_rows.shape[0]
    scores = (
        lax.dot_general(
            query_rows, key_rows, (((1,), (1,)), ((), ())), preferred_element_type=jnp.float32
        )
        * softmax_scale
    )
    scores = scores.reshape(visible.shape[0], -1, key_count)
    seen = visible[:, None, :]
    maxima = jnp.max(jnp.where(seen, scores, lowest_score), axis=-1)
    expons = jnp.where(seen, jnp.exp(scores - maxima[..., None]), 0.0)
    sums = jnp.sum(expons, axis=-1)
    weights = expons.astype(jnp.bfloat16).reshape(-1, key_count)
    weighted = jnp.dot(weights, key_rows[:, :rank_dim], preferred_element_type=jnp.float32)
    return (maxima.reshape(-1), sums.reshape(-1), weighted)


def body(
    queries, new_latent, own_cache, prompt_pool, uv_weight, owner, route, prompt_len, page_table
):
    requests, num_steps, head_dev, latent = queries.shape
    rank_dim = uv_weight.shape[1]
    vhead_dim = uv_weight.shape[2]
    page_len = prompt_pool.shape[2]
    num_pages = page_table.shape[0]
    row_count = requests * num_steps * head_dev
    query_rows = queries.reshape(row_count, latent)
    query_block = queries.reshape(requests, num_steps * head_dev, latent)
    active = route[0] > 0
    local_keys = jnp.concatenate([own_cache, new_latent], axis=1)
    local_scores = (
        jnp.einsum("rqc,rkc->rqk", query_block, local_keys, preferred_element_type=jnp.float32)
        * softmax_scale
    )
    step_of_row = jnp.arange(num_steps * head_dev, dtype=jnp.int32) // head_dev
    new_seen = jnp.arange(num_steps, dtype=jnp.int32)[None, :] <= step_of_row[:, None]
    own_seen = jnp.ones((num_steps * head_dev, own_cache.shape[1]), bool)
    local_seen = jnp.concatenate([own_seen, new_seen], axis=1)[None, :, :]
    local_max = jnp.max(jnp.where(local_seen, local_scores, lowest_score), axis=-1)
    local_exp = jnp.where(local_seen, jnp.exp(local_scores - local_max[..., None]), 0.0)
    local_sums = jnp.sum(local_exp, axis=-1)
    local_weighted = jnp.einsum(
        "rqk,rkc->rqc",
        local_exp.astype(jnp.bfloat16),
        local_keys[:, :, :rank_dim],
        preferred_element_type=jnp.float32,
    )
    local_stats = (
        local_max.reshape(-1),
        local_sums.reshape(-1),
        local_weighted.reshape(row_count, rank_dim),
    )
    slots = jnp.arange(num_pages, dtype=jnp.int32)
    matches = (page_table[:, None] == slots[None, :]).astype(jnp.int32)
    logical = jnp.sum(matches * slots[:, None], axis=0)
    offsets = jnp.arange(page_len, dtype=jnp.int32)
    group_ids = jnp.arange(owner.shape[0], dtype=jnp.int32)
    root = jnp.sum(jnp.where(owner == 0, group_ids, 0))
    shard = from_root(prompt_pool, "group", root)
    arrived = lax.all_gather(shard, "head", axis=1, tiled=True)
    firsts = logical * page_len
    places = (firsts[:, None] + offsets[None, :]).reshape(-1)
    visible = (places[None, :] < prompt_len[:, None]) & active
    prompt_stats = block_stats(query_rows, arrived.reshape(-1, latent), visible, rank_dim)
    merged = combine_stats(prompt_stats, local_stats)
    latent_out = (merged[2] / merged[1][:, None]).astype(jnp.bfloat16)
    latent_out = latent_out.reshape(requests, num_steps, head_dev, rank_dim)
    attended = jnp.einsum(
        "rthc,hcv->rthv", latent_out, uv_weight, preferred_element_type=jnp.float32
    )
    return attended.reshape(requests, num_steps, head_dev * vhead_dim).astype(jnp.bfloat16)


def solution(mesh):
    placed = (
        P("group", None, "head", None),
        P("group", None, None),
        P("group", None, None),
        P("group", "head", None, None),
        P("head", None, None),
        P(),
        P("group"),
        P("group"),
        P(),
    )
    return jax.shard_map(
        body, mesh=mesh, in_specs=placed, out_specs=P("group", None, "head"), check_vma=False
    )
```

profile of v0, /device:TPU:1, one launch (start us, length us, event | category | flops | bytes accessed | tf_op | source)
XLA Modules:
  0.0 453.9 jit_solution(7866492182819910126)
XLA Ops:
  6.5 1.4 fusion.39
  8.6 1.6 bitcast_select_fusion.1
  10.3 334.6 %all-reduce.3.cloned.1.call-done = bf16[1,2,64,576]{3,2,0,1:T(8,128)(2,1)} async-done(((bf16[1,2,64,576]{3,2,0,1:T(8,128)(2,1)}), bf16[1,2,64,576]{3,2,0,1:T(8,128)(2,1)}) %all-reduce.3.cloned.1.call-update) | async-done | bytes 147472 | tf_op jit(solution)/shard_map/psum | solution.py:12
  345.5 0.7 select_reduce_fusion.1
  346.3 0.1 iota_add_fusion
  346.3 0.1 add.40
  346.4 0.1 iota_compare_fusion
  346.5 0.1 concatenate.6
  346.6 1.4 constant_dynamic-update-slice_fusion.1
  348.0 0.1 constant_dynamic-update-slice_fusion
  348.2 0.7 select_reduce_fusion
  348.9 0.1 reshape.139
  349.0 0.4 fusion.31
  349.4 0.1 compare_and_fusion
  349.6 0.5 broadcast_in_dim.59
  350.1 4.2 copy.24
  354.3 1.8 fusion.18
  356.1 76.9 %all-gather.2.cloned.1.call-done = bf16[1,32,64,576]{3,2,0,1:T(8,128)(2,1)} async-done(((bf16[1,2,64,576]{3,2,0,1:T(8,128)(2,1)}), bf16[1,32,64,576]{3,2,0,1:T(8,128)(2,1)}) %all-gather.2.cloned.1.call-update) | async-done | bytes 2359312 | tf_op jit(solution)/shard_map/all_gather | solution.py:84
  433.0 6.7 %fusion = (f32[1024]{0:T(1024)S(1)}, f32[2048,1024]{1,0:T(8,128)S(1)}) fusion(pred[1024,2048]{0,1:T(32,128)(4,1)} %copy.24, bf16[2048,576]{1,0:T(8,128)(2,1)} %bitcast.56, bf16[1024,576]{1,0:T(8,128)(2,1)S(1)} %bitcast.54), kind=kOutput, calls=%fused_computation.2 | convolution fusion | flops 2422209536 | bytes 14028800 | tf_op jit(solution)/shard_map/dot_general | solution.py:27
  439.8 2.3 fusion.3
  442.1 2.6 fusion.13
  444.8 1.3 fusion.28
  446.1 0.2 copy.29
  446.3 0.8 reshape.144
  (22 shorter events, 0.3 us)
Async XLA Ops:
  6.5 341.6 %copy-start = (bf16[32,4,8,576]{3,2,1,0:T(8,128)(2,1)S(1)}, bf16[32,4,8,576]{3,2,1,0:T(8,128)(2,1)}, u32[]{:S(2)}) copy-start(bf16[32,4,8,576]{3,2,1,0:T(8,128)(2,1)} %param.9) | copy-start | bytes 3538948
  6.5 341.5 %copy-start.3 = (bf16[32,4,576]{2,1,0:T(4,128)(2,1)S(1)}, bf16[32,4,576]{2,1,0:T(4,128)(2,1)}, u32[]{:S(2)}) copy-start(bf16[32,4,576]{2,1,0:T(4,128)(2,1)} %param.10) | copy-start | bytes 442372
  6.5 338.3 %all-reduce.3.cloned.1.call-start = ((), (), s32[]{:S(2)}) async-start(), calls=%async_computation | async-start | bytes 327680 | tf_op jit(solution)/shard_map/psum | solution.py:12
  10.2 422.8 %all-gather.2.cloned.1.call-start = ((), (), s32[]{:S(2)}) async-start(), calls=%async_computation.1 | async-start | bytes 2785280 | tf_op jit(solution)/shard_map/all_gather | solution.py:84
  348.2 1.3 copy-start.4
  433.0 6.7 %copy-start.1 = (pred[1024,2048]{0,1:T(32,128)(4,1)S(1)}, pred[1024,2048]{0,1:T(32,128)(4,1)}, u32[]{:S(2)}) copy-start(pred[1024,2048]{0,1:T(32,128)(4,1)} %copy.24) | copy-start | bytes 6291460
  439.8 2.3 copy-start.2
  439.8 2.4 copy-start.5
  442.1 2.7 copy-start.6
Sparse Core Ops, SparseCore 0:
  10.3 334.4 all-reduce.2
  347.1 85.8 all-gather.1
where the time goes:
time: 463 us; the launch traced here: 454 us
  waiting for transfers between devices  411 us (89%)
  between operations  14.8 us (3%)
  matrix products  13.2 us (3%)
  local copies, waits for them, and re-layouts  7.66 us (2%)
  other arithmetic  6.69 us (1%)
    psum x1, waiting for transfers between devices, from_root(): return lax.psum(jnp.where(mine, value, jnp.zeros_like(value)), axis)  335 us
    all_gather x1, waiting for transfers between devices, body(): arrived = lax.all_gather(shard, 'head', axis=1, tiled=True)  76.9 us
  transfers between devices with their start and end apart: 2, of which 2 were waited for; matrix products, arithmetic and copies ran while one was open for 2% of the time, Pallas kernels for 0%

commit v1 on v0

v1 whole, which is shorter than its diff:
```python
import functools

import jax
import jax.numpy as jnp
from jax import lax
from jax.experimental import pallas as pl
from jax.experimental.pallas import tpu as pltpu
from jax.sharding import Mesh, PartitionSpec as P
import numpy as np

softmax_scale = 192.0 ** (-0.5)
lowest_score = -1e30
log2_scale = softmax_scale * 1.4426950408889634

axis_names = ("zh", "y", "c", "x", "zl")
axis_sizes = (4, 4, 2, 4, 4)
group_axes = ("zh", "y", "c")
head_axes = ("x", "zl")


def moves(change):
    pairs = []
    for index, place in enumerate(np.ndindex(*axis_sizes)):
        pairs.append((index, int(np.ravel_multi_index(change(*place), axis_sizes))))
    return pairs


def shift_high(steps):
    return moves(lambda zh, y, c, x, zl: ((zh + steps) % 4, y, c, x, zl))


def gathered(value, axes, count):
    tiled = jnp.broadcast_to(value[None], (count,) + value.shape)
    return lax.all_to_all(tiled, axes, 0, 0, tiled=True)


def keys_stats(query, keys, places, lens_ref, first_request, rows_per_request):
    scores = lax.dot_general(
        query, keys, (((1,), (1,)), ((), ())), preferred_element_type=jnp.float32
    )
    rows, key_count = scores.shape
    parts = []
    for number in range(rows // rows_per_request):
        seen = places < lens_ref[first_request + number]
        part = scores[number * rows_per_request : (number + 1) * rows_per_request]
        part = part.reshape(rows_per_request // 8, 8, key_count)
        parts.append(jnp.where(seen[None], part, lowest_score).reshape(-1, key_count))
    scores = jnp.concatenate(parts, axis=0)
    maxima = jnp.max(scores, axis=1, keepdims=True)
    expons = jnp.exp2(scores * log2_scale - maxima * log2_scale)
    sums = jnp.sum(expons, axis=1, keepdims=True)
    return maxima, sums, expons.astype(jnp.bfloat16)


def first_kernel(rank_dim, rows_per_request, lens_ref, query_ref, keys_ref, places_ref,
                 max_ref, sum_ref, acc_ref):
    block = query_ref.shape[0]
    start = pl.program_id(0) * (block // rows_per_request)
    maxima, sums, weights = keys_stats(
        query_ref[...], keys_ref[...], places_ref[...], lens_ref, start, rows_per_request
    )
    acc_ref[...] = jnp.dot(
        weights, keys_ref[:, :rank_dim], preferred_element_type=jnp.float32
    )
    max_ref[...] = jnp.broadcast_to(maxima, max_ref.shape)
    sum_ref[...] = jnp.broadcast_to(sums, sum_ref.shape)


def last_kernel(rank_dim, rows_per_request, heads, lens_ref, query_ref, keys_ref, places_ref,
                max_ref, sum_ref, acc_ref, local_max_ref, local_sum_ref, local_acc_ref,
                uv_ref, out_ref, latent_ref):
    step = pl.program_id(0)
    block = query_ref.shape[0]
    start = step * (block // rows_per_request)
    maxima, sums, weights = keys_stats(
        query_ref[...], keys_ref[...], places_ref[...], lens_ref, start, rows_per_request
    )
    weighted = jnp.dot(
        weights, keys_ref[:, :rank_dim], preferred_element_type=jnp.float32
    )
    first_max = max_ref[:, :1]
    local_max = local_max_ref[...]
    peak = jnp.maximum(jnp.maximum(maxima, first_max), local_max)
    factor = jnp.exp2((maxima - peak) * log2_scale)
    first_factor = jnp.exp2((first_max - peak) * log2_scale)
    local_factor = jnp.exp2((local_max - peak) * log2_scale)
    total = sums * factor + sum_ref[:, :1] * first_factor + local_sum_ref[...] * local_factor
    inverse = 1.0 / total
    latent = (
        weighted * (factor * inverse)
        + acc_ref[...] * (first_factor * inverse)
        + local_acc_ref[...] * (local_factor * inverse)
    )
    latent = latent.astype(jnp.bfloat16).astype(jnp.float32)
    at = pl.ds(pl.multiple_of(step * block, block), block)
    for part in range(latent_ref.shape[0]):
        latent_ref[part, at, :] = latent[:, part * 128 : (part + 1) * 128]

    @pl.when(step == pl.num_programs(0) - 1)
    def project():
        tokens = out_ref.shape[0]
        vhead = uv_ref.shape[2]
        for head in range(heads):
            rows = jnp.concatenate(
                [
                    latent_ref[part, pl.ds(head, tokens, stride=heads), :].astype(jnp.bfloat16)
                    for part in range(latent_ref.shape[0])
                ],
                axis=1,
            )
            out_ref[:, head * vhead : (head + 1) * vhead] = jnp.dot(
                rows, uv_ref[head], preferred_element_type=jnp.float32
            ).astype(jnp.bfloat16)


def body(
    queries, new_latent, own_cache, prompt_pool, uv_weight, owner, route, prompt_len, page_table
):
    requests, num_steps, head_dev, latent = queries.shape
    rank_dim = uv_weight.shape[1]
    vhead_dim = uv_weight.shape[2]
    own_pages, page_len = prompt_pool.shape[1:3]
    num_pages = page_table.shape[0]
    row_count = requests * num_steps * head_dev
    rows_per_request = num_steps * head_dev
    query_rows = queries.reshape(row_count, latent)
    query_block = queries.reshape(requests, rows_per_request, latent)

    group_ids = jnp.arange(owner.shape[0], dtype=jnp.int32)
    root = jnp.sum(jnp.where(owner == 0, group_ids, 0))
    root_high = root // 8
    root_piece = root % 8

    pieces = prompt_pool.reshape(8, own_pages * page_len // 8, latent)
    pieces = lax.all_to_all(pieces, ("y", "c"), 0, 0, tiled=True)
    piece = lax.dynamic_index_in_dim(pieces, root_piece, 0, keepdims=False)
    up = lax.ppermute(piece, axis_names, shift_high(1))
    down = lax.ppermute(piece, axis_names, shift_high(3))
    across = lax.ppermute(piece, axis_names, shift_high(2))
    apart = (lax.axis_index("zh") - root_high) % 4
    piece = jnp.where(
        apart == 0, piece, jnp.where(apart == 1, up, jnp.where(apart == 3, down, across))
    )
    run = gathered(piece, "zl", 4)
    half = gathered(run.reshape(-1, latent), ("x", "y"), 16)
    other = lax.ppermute(half, "c", [(0, 1), (1, 0)]).reshape(-1, latent)
    half = half.reshape(-1, latent)

    own_scores = jnp.einsum(
        "rqc,rkc->rqk", query_block, own_cache, preferred_element_type=jnp.float32
    )
    new_scores = jnp.einsum(
        "rqc,rkc->rqk", query_block, new_latent, preferred_element_type=jnp.float32
    )
    step_of_row = jnp.arange(rows_per_request, dtype=jnp.int32) // head_dev
    new_seen = jnp.arange(num_steps, dtype=jnp.int32)[None, :] <= step_of_row[:, None]
    new_scores = jnp.where(new_seen[None], new_scores, lowest_score)
    local_max = jnp.maximum(jnp.max(own_scores, axis=-1), jnp.max(new_scores, axis=-1))
    own_exp = jnp.exp2((own_scores - local_max[..., None]) * log2_scale)
    new_exp = jnp.exp2((new_scores - local_max[..., None]) * log2_scale)
    local_sums = jnp.sum(own_exp, axis=-1) + jnp.sum(new_exp, axis=-1)
    local_weighted = jnp.einsum(
        "rqk,rkc->rqc", own_exp.astype(jnp.bfloat16), own_cache[:, :, :rank_dim],
        preferred_element_type=jnp.float32,
    ) + jnp.einsum(
        "rqk,rkc->rqc", new_exp.astype(jnp.bfloat16), new_latent[:, :, :rank_dim],
        preferred_element_type=jnp.float32,
    )
    local_max = local_max.reshape(row_count, 1)
    local_sums = local_sums.reshape(row_count, 1)
    local_weighted = local_weighted.reshape(row_count, rank_dim)

    slots = jnp.arange(num_pages, dtype=jnp.int32)
    matches = (page_table[:, None] == slots[None, :]).astype(jnp.int32)
    logical = jnp.sum(matches * slots[:, None], axis=0)
    core = lax.axis_index("c")
    piece_rows = own_pages * page_len // 8
    firsts = jnp.broadcast_to(
        logical.reshape(4, 1, 4, own_pages, 1) * page_len, (4, 1, 4, own_pages, 1)
    )
    firsts = jnp.moveaxis(firsts, 3, 1).reshape(4, own_pages, 1, 4, 1)
    within = (
        (jnp.arange(2, dtype=jnp.int32) * 2)[None, None, :, None, None] * piece_rows
        + jnp.arange(piece_rows, dtype=jnp.int32)[None, None, None, None, :]
    )
    places = (firsts + within).reshape(1, -1)
    key_count = places.shape[1]
    places = jnp.broadcast_to(places, (8, key_count))
    own_places = places + core * piece_rows
    other_places = places + (1 - core) * piece_rows
    lens = jnp.where(route[0] > 0, prompt_len, 0)

    block = 256
    steps = row_count // block
    whole = lambda shape: pl.BlockSpec(shape, lambda i, lens: (0,) * len(shape))
    rows = lambda width: pl.BlockSpec((block, width), lambda i, lens: (i, 0))
    cost = pl.CostEstimate(
        flops=2 * row_count * key_count * (latent + rank_dim),
        bytes_accessed=2 * (row_count + key_count) * latent + 4 * row_count * rank_dim,
        transcendentals=row_count * key_count,
    )
    params = pltpu.CompilerParams(vmem_limit_bytes=24 * 1024 * 1024)
    first = pl.pallas_call(
        functools.partial(first_kernel, rank_dim, rows_per_request),
        grid_spec=pltpu.PrefetchScalarGridSpec(
            num_scalar_prefetch=1,
            grid=(steps,),
            in_specs=[rows(latent), whole((key_count, latent)), whole((8, key_count))],
            out_specs=[rows(128), rows(128), rows(rank_dim)],
        ),
        out_shape=[
            jax.ShapeDtypeStruct((row_count, 128), jnp.float32),
            jax.ShapeDtypeStruct((row_count, 128), jnp.float32),
            jax.ShapeDtypeStruct((row_count, rank_dim), jnp.float32),
        ],
        compiler_params=params,
        cost_estimate=cost,
    )
    first_max, first_sum, first_acc = first(lens, query_rows, half, own_places)
    last = pl.pallas_call(
        functools.partial(last_kernel, rank_dim, rows_per_request, head_dev),
        grid_spec=pltpu.PrefetchScalarGridSpec(
            num_scalar_prefetch=1,
            grid=(steps,),
            in_specs=[
                rows(latent), whole((key_count, latent)), whole((8, key_count)),
                rows(128), rows(128), rows(rank_dim), rows(1), rows(1), rows(rank_dim),
                whole(uv_weight.shape),
            ],
            out_specs=whole((row_count // head_dev, head_dev * vhead_dim)),
            scratch_shapes=[pltpu.VMEM((rank_dim // 128, row_count, 128), jnp.float32)],
        ),
        out_shape=jax.ShapeDtypeStruct((row_count // head_dev, head_dev * vhead_dim), jnp.bfloat16),
        compiler_params=params,
        cost_estimate=cost,
    )
    attended = last(
        lens, query_rows, other, other_places, first_max, first_sum, first_acc,
        local_max, local_sums, local_weighted, uv_weight,
    )
    return attended.reshape(requests, num_steps, head_dev * vhead_dim)


def solution(mesh):
    fine = Mesh(mesh.devices.reshape(axis_sizes), axis_names)
    placed = (
        P(group_axes, None, head_axes, None),
        P(group_axes, None, None),
        P(group_axes, None, None),
        P(group_axes, head_axes, None, None),
        P(head_axes, None, None),
        P(),
        P(group_axes),
        P(group_axes),
        P(),
    )
    return jax.shard_map(
        body, mesh=fine, in_specs=placed, out_specs=P(group_axes, None, head_axes), check_vma=False
    )
```

time: 463 us -> 95.9 us (0.21); the launches traced: 454 us -> 95.2 us
  waiting for transfers between devices: 411 us -> 21.2 us
  starting transfers between devices: 0.04 us -> 45.4 us
  Pallas kernels: 0 us -> 13.9 us
  between operations: 14.8 us -> 3.55 us
  matrix products: 13.2 us -> 4.6 us
    psum x1 -> x0, waiting for transfers between devices: 335 us -> none  [from_root(): return lax.psum(jnp.where(mine, value, jnp.zeros_like(value)), axis)]
    all_gather x1 -> x0, waiting for transfers between devices: 76.9 us -> none  [body(): arrived = lax.all_gather(shard, 'head', axis=1, tiled=True)]
    ppermute x0 -> x4, starting transfers between devices: none -> 26.6 us  [the longest x1 10.3 us: body(): across = lax.ppermute(piece, axis_names, shift_high(2))]
    all_to_all x0 -> x3, waiting for transfers between devices: none -> 19.1 us  [the longest x2 17.5 us: gathered(): return lax.all_to_all(tiled, axes, 0, 0, tiled=True)]
    all_to_all x0 -> x3, starting transfers between devices: none -> 18.8 us  [the longest x1 10.2 us: body(): pieces = lax.all_to_all(pieces, ('y', 'c'), 0, 0, tiled=True)]
    pallas_call x0 -> x2, Pallas kernels: none -> 13.9 us  [the longest x1 7.46 us: body(): last(lens, query_rows, other, other_places, first_max, first_sum, first_a...]
    dot_general x5 -> x4, matrix products: 13.2 us -> 4.6 us  [the longest x1 1.88 us: body(): jnp.einsum('rqc,rkc->rqk', query_block, own_cache, preferred_element_type...]
  transfers between devices with their start and end apart: 2 -> 7, of which waited for: 2 -> 4; matrix products, arithmetic and copies ran while one was open for 2% -> 9% of each run, Pallas kernels for 0% -> 7%
where the time goes in v1:
time: 95.9 us; the launch traced here: 95.2 us
  starting transfers between devices  45.4 us (47%)
  waiting for transfers between devices  21.2 us (22%)
  Pallas kernels  13.9 us (14%)
  matrix products  4.6 us (5%)
  local copies, waits for them, and re-layouts  4.17 us (4%)
  between operations  3.55 us (4%)
  other arithmetic  2.44 us (3%)
    all_to_all x2, waiting for transfers between devices, gathered(): return lax.all_to_all(tiled, axes, 0, 0, tiled=True)  17.5 us
    ppermute x1, starting transfers between devices, body(): across = lax.ppermute(piece, axis_names, shift_high(2))  10.3 us
    all_to_all x1, starting transfers between devices, body(): pieces = lax.all_to_all(pieces, ('y', 'c'), 0, 0, tiled=True)  10.2 us
    all_to_all x2, starting transfers between devices, gathered(): return lax.all_to_all(tiled, axes, 0, 0, tiled=True)  8.62 us
    pallas_call x1, Pallas kernels, body(): last(lens, query_rows, other, other_places, first_max, first_sum, first_a...  7.46 us
    pallas_call x1, Pallas kernels, body(): first_max, first_sum, first_acc = first(lens, query_rows, half, own_places)  6.45 us
    ppermute x1, starting transfers between devices, body(): other = lax.ppermute(half, 'c', [(0, 1), (1, 0)]).reshape(-1, latent)  6.17 us
    ppermute x1, starting transfers between devices, body(): down = lax.ppermute(piece, axis_names, shift_high(3))  5.56 us
  transfers between devices with their start and end apart: 7, of which 4 were waited for; matrix products, arithmetic and copies ran while one was open for 9% of the time, Pallas kernels for 7%

profile of v1, /device:TPU:1, one launch (start us, length us, event | category | flops | bytes accessed | tf_op | source)
XLA Modules:
  0.0 95.2 jit_solution(16753555346074635261)
XLA Ops:
  0.0 10.2 %all-to-all-start = ((bf16[8,16,576]{2,1,0:T(8,128)(2,1)}), bf16[8,16,576]{2,1,0:T(8,128)(2,1)S(1)}, u32[]{:S(2)}, u32[]{:S(2)}) async-start(bf16[8,16,576]{2,1,0:T(8,128)(2,1)} %bitcast.30), calls=%async_computation | async-start | bytes 327680 | tf_op jit(solution)/shard_map/all_to_all | solution.py:135
  10.2 1.3 %fusion.20 = s32[]{:T(128)} fusion(s32[32]{0:T(128)} %param.14), kind=kLoop, calls=%fused_computation.33 | loop fusion | flops 95 | bytes 132 | tf_op jit(solution)/shard_map/reduce_sum | solution.py:130
  13.4 0.7 select_reduce_fusion
  14.2 1.6 %all-to-all-done = bf16[8,16,576]{2,1,0:T(8,128)(2,1)S(1)} async-done(((bf16[8,16,576]{2,1,0:T(8,128)(2,1)}), bf16[8,16,576]{2,1,0:T(8,128)(2,1)S(1)}, u32[]{:S(2)}, u32[]{:S(2)}) %all-to-all-start) | async-done | bytes 147488 | tf_op jit(solution)/shard_map/all_to_all | solution.py:135
  15.8 4.6 %collective-permute-start = (bf16[16,576]{1,0:T(8,128)(2,1)S(1)}, bf16[16,576]{1,0:T(8,128)(2,1)S(1)}, u32[]{:S(2)}, u32[]{:S(2)}) collective-permute-start(bf16[16,576]{1,0:T(8,128)(2,1)S(1)} %dynamic-slice_bitcast_fusion), channel_id=1, source_target_pairs={{0,128},{1,129},{2,130},{3,131},{4,132},{5,133},{6,134},{7,135},{8... | collective-permute-start | bytes 55304 | tf_op jit(solution)/shard_map/ppermute | solution.py:137
  20.4 5.6 %collective-permute-start.1 = (bf16[16,576]{1,0:T(8,128)(2,1)S(1)}, bf16[16,576]{1,0:T(8,128)(2,1)S(1)}, u32[]{:S(2)}, u32[]{:S(2)}) collective-permute-start(bf16[16,576]{1,0:T(8,128)(2,1)S(1)} %dynamic-slice_bitcast_fusion), channel_id=1, source_target_pairs={{0,384},{1,385},{2,386},{3,387},{4,388},{5,389},{6,390},{7,391},{8... | collective-permute-start | bytes 55304 | tf_op jit(solution)/shard_map/ppermute | solution.py:138
  25.9 10.3 %collective-permute-start.2 = (bf16[16,576]{1,0:T(8,128)(2,1)S(1)}, bf16[16,576]{1,0:T(8,128)(2,1)S(1)}, u32[]{:S(2)}, u32[]{:S(2)}) collective-permute-start(bf16[16,576]{1,0:T(8,128)(2,1)S(1)} %dynamic-slice_bitcast_fusion), channel_id=1, source_target_pairs={{0,256},{1,257},{2,258},{3,259},{4,260},{5,261},{6,262},{7,263},{8... | collective-permute-start | bytes 55304 | tf_op jit(solution)/shard_map/ppermute | solution.py:139
  37.1 2.1 %collective-permute-done.2 = bf16[16,576]{1,0:T(8,128)(2,1)S(1)} collective-permute-done((bf16[16,576]{1,0:T(8,128)(2,1)S(1)}, bf16[16,576]{1,0:T(8,128)(2,1)S(1)}, u32[]{:S(2)}, u32[]{:S(2)}) %collective-permute-start.2) | collective-permute-done | bytes 18464 | tf_op jit(solution)/shard_map/ppermute | solution.py:139
  39.2 0.6 broadcast_in_dim.28
  39.9 3.3 %all-to-all-start.1 = ((bf16[4,16,576]{2,1,0:T(8,128)(2,1)}), bf16[4,16,576]{2,1,0:T(8,128)(2,1)S(1)}, u32[]{:S(2)}, u32[]{:S(2)}) async-start(bf16[4,16,576]{2,1,0:T(8,128)(2,1)} %broadcast_in_dim.28), calls=%async_computation.1 | async-start | bytes 163840 | tf_op jit(solution)/shard_map/all_to_all | solution.py:34
  43.3 4.5 %all-to-all-done.1 = bf16[4,16,576]{2,1,0:T(8,128)(2,1)S(1)} async-done(((bf16[4,16,576]{2,1,0:T(8,128)(2,1)}), bf16[4,16,576]{2,1,0:T(8,128)(2,1)S(1)}, u32[]{:S(2)}, u32[]{:S(2)}) %all-to-all-start.1) | async-done | bytes 73760 | tf_op jit(solution)/shard_map/all_to_all | solution.py:34
  47.8 1.2 %broadcast_in_dim.30 = bf16[16,64,576]{2,1,0:T(8,128)(2,1)} broadcast(bf16[64,576]{1,0:T(8,128)(2,1)S(1)} %bitcast.29), dimensions={1,2} | broadcast | bytes 1253376 | tf_op jit(solution)/shard_map/broadcast_in_dim | solution.py:33
  49.0 5.3 %all-to-all-start.2 = ((bf16[16,64,576]{2,1,0:T(8,128)(2,1)}), bf16[16,64,576]{2,1,0:T(8,128)(2,1)}, u32[]{:S(2)}, u32[]{:S(2)}) async-start(bf16[16,64,576]{2,1,0:T(8,128)(2,1)} %broadcast_in_dim.30), calls=%async_computation.2 | async-start | bytes 2621440 | tf_op jit(solution)/shard_map/all_to_all | solution.py:34
  55.2 0.5 fusion.24
  55.8 1.9 %fusion.23 = (f32[32,32]{1,0:T(8,128)S(1)}, f32[32,32,32]{1,2,0:T(8,128)S(1)}) fusion(bf16[32,32,576]{2,1,0:T(8,128)(2,1)} %param.11, bf16[32,4,8,576]{3,2,1,0:T(8,128)(2,1)S(1)} %copy-done), kind=kOutput, calls=%fused_computation.38 | convolution fusion | flops 37780480 | bytes 2494464 | tf_op jit(solution)/shard_map/rqc,rkc->rqk/dot_general | solution.py:149
  57.7 0.5 max.19.local_max_ref
  58.4 13.0 %all-to-all-done.2 = bf16[16,64,576]{2,1,0:T(8,128)(2,1)} async-done(((bf16[16,64,576]{2,1,0:T(8,128)(2,1)}), bf16[16,64,576]{2,1,0:T(8,128)(2,1)}, u32[]{:S(2)}, u32[]{:S(2)}) %all-to-all-start.2) | async-done | bytes 1179680 | tf_op jit(solution)/shard_map/all_to_all | solution.py:34
  71.3 6.2 %collective-permute-start.3 = (bf16[16,64,576]{2,1,0:T(8,128)(2,1)}, bf16[16,64,576]{2,1,0:T(8,128)(2,1)}, u32[]{:S(2)}, u32[]{:S(2)}) collective-permute-start(bf16[16,64,576]{2,1,0:T(8,128)(2,1)} %all-to-all-done.2), channel_id=1, source_target_pairs={{0,16},{16,0},{1,17},{17,1},{2,18},{18,2},{3,19},{19,3},{4,20},{20... | collective-permute-start | bytes 3538952 | tf_op jit(solution)/shard_map/ppermute | solution.py:146
  77.6 0.5 add.106.local_sum_ref
  78.2 1.7 %fusion.7 = f32[32,32,512]{2,1,0:T(8,128)S(1)} fusion(bf16[32,32,576]{2,1,0:T(8,128)(2,1)} %param.11, f32[32,32,32]{1,2,0:T(8,128)S(1)} %get-tuple-element.14, f32[32,32]{1,0:T(8,128)S(1)} %max.17), kind=kOutput, calls=%fused_computation.6 | convolution fusion | flops 33652736 | bytes 3280896 | tf_op jit(solution)/shard_map/rqk,rkc->rqc/dot_general | solution.py:162
  79.9 0.5 convolution_add_fusion
  80.5 6.4 %shard_map.91 = (f32[1024,128]{1,0:T(8,128)S(1)}, f32[1024,128]{1,0:T(8,128)S(1)}, f32[1024,512]{1,0:T(8,128)S(1)}) custom-call(s32[32]{0:T(128)S(1)} %broadcast_select_fusion.lens_ref, bf16[1024,576]{1,0:T(8,128)(2,1)S(1)} %bitcast.27, bf16[1024,576]{1,0:T(8,128)(2,1)} %bitcast.8.keys_ref, s32[8,1024]{1,0:T(8,128)S(1)} %broadcast_in_dim.53.places_ref), custom_call_target="tpu_custom_call" | custom-call | flops 2281701376 | bytes 4456448 | tf_op jit(solution)/shard_map/pallas_call | solution.py:219
  86.9 7.5 %shard_map.92 = bf16[128,1024]{1,0:T(8,128)(2,1)S(1)} custom-call(s32[32]{0:T(128)S(1)} %broadcast_select_fusion.lens_ref, bf16[1024,576]{1,0:T(8,128)(2,1)S(1)} %bitcast.28, bf16[1024,576]{1,0:T(8,128)(2,1)} %bitcast.5.keys_ref, s32[8,1024]{1,0:T(8,128)S(1)} %broadcast_in_dim.52.places_ref, f32[1024,128]{1,0:T(8,128)S(1)} %get-tuple-element.8.max_ref, ...), custom_call_target="tpu_custom_call" | custom-call | flops 2281701376 | bytes 4456448 | tf_op jit(solution)/shard_map/pallas_call | solution.py:237
  94.4 0.8 reshape.169
  (30 shorter events, 0.8 us)
Async XLA Ops:
  0.0 15.8 %all-to-all-start = ((bf16[8,16,576]{2,1,0:T(8,128)(2,1)}), bf16[8,16,576]{2,1,0:T(8,128)(2,1)S(1)}, u32[]{:S(2)}, u32[]{:S(2)}) async-start(bf16[8,16,576]{2,1,0:T(8,128)(2,1)} %bitcast.30), calls=%async_computation | async-start | bytes 327680 | tf_op jit(solution)/shard_map/all_to_all | solution.py:135
  15.8 21.3 %collective-permute-start = (bf16[16,576]{1,0:T(8,128)(2,1)S(1)}, bf16[16,576]{1,0:T(8,128)(2,1)S(1)}, u32[]{:S(2)}, u32[]{:S(2)}) collective-permute-start(bf16[16,576]{1,0:T(8,128)(2,1)S(1)} %dynamic-slice_bitcast_fusion), channel_id=1, source_target_pairs={{0,128},{1,129},{2,130},{3,131},{4,132},{5,133},{6,134},{7,135},{8... | collective-permute-start | bytes 55304 | tf_op jit(solution)/shard_map/ppermute | solution.py:137
  20.4 16.7 %collective-permute-start.1 = (bf16[16,576]{1,0:T(8,128)(2,1)S(1)}, bf16[16,576]{1,0:T(8,128)(2,1)S(1)}, u32[]{:S(2)}, u32[]{:S(2)}) collective-permute-start(bf16[16,576]{1,0:T(8,128)(2,1)S(1)} %dynamic-slice_bitcast_fusion), channel_id=1, source_target_pairs={{0,384},{1,385},{2,386},{3,387},{4,388},{5,389},{6,390},{7,391},{8... | collective-permute-start | bytes 55304 | tf_op jit(solution)/shard_map/ppermute | solution.py:138
  25.9 13.3 %collective-permute-start.2 = (bf16[16,576]{1,0:T(8,128)(2,1)S(1)}, bf16[16,576]{1,0:T(8,128)(2,1)S(1)}, u32[]{:S(2)}, u32[]{:S(2)}) collective-permute-start(bf16[16,576]{1,0:T(8,128)(2,1)S(1)} %dynamic-slice_bitcast_fusion), channel_id=1, source_target_pairs={{0,256},{1,257},{2,258},{3,259},{4,260},{5,261},{6,262},{7,263},{8... | collective-permute-start | bytes 55304 | tf_op jit(solution)/shard_map/ppermute | solution.py:139
  39.9 7.9 %all-to-all-start.1 = ((bf16[4,16,576]{2,1,0:T(8,128)(2,1)}), bf16[4,16,576]{2,1,0:T(8,128)(2,1)S(1)}, u32[]{:S(2)}, u32[]{:S(2)}) async-start(bf16[4,16,576]{2,1,0:T(8,128)(2,1)} %broadcast_in_dim.28), calls=%async_computation.1 | async-start | bytes 163840 | tf_op jit(solution)/shard_map/all_to_all | solution.py:34
  49.0 6.2 %copy-start = (bf16[32,4,8,576]{3,2,1,0:T(8,128)(2,1)S(1)}, bf16[32,4,8,576]{3,2,1,0:T(8,128)(2,1)}, u32[]{:S(2)}) copy-start(bf16[32,4,8,576]{3,2,1,0:T(8,128)(2,1)} %param.9) | copy-start | bytes 3538948
  49.0 6.2 %copy-start.2 = (bf16[32,4,576]{2,1,0:T(4,128)(2,1)S(1)}, bf16[32,4,576]{2,1,0:T(4,128)(2,1)}, u32[]{:S(2)}) copy-start(bf16[32,4,576]{2,1,0:T(4,128)(2,1)} %param.10) | copy-start | bytes 442372
  49.0 22.3 %all-to-all-start.2 = ((bf16[16,64,576]{2,1,0:T(8,128)(2,1)}), bf16[16,64,576]{2,1,0:T(8,128)(2,1)}, u32[]{:S(2)}, u32[]{:S(2)}) async-start(bf16[16,64,576]{2,1,0:T(8,128)(2,1)} %broadcast_in_dim.30), calls=%async_computation.2 | async-start | bytes 2621440 | tf_op jit(solution)/shard_map/all_to_all | solution.py:34
  57.6 20.6 %copy-start.3 = (s32[32]{0:T(128)S(1)}, s32[32]{0:T(128)}, u32[]{:S(2)}) copy-start(s32[32]{0:T(128)} %param.16) | copy-start | bytes 388
  71.3 15.6 %collective-permute-start.3 = (bf16[16,64,576]{2,1,0:T(8,128)(2,1)}, bf16[16,64,576]{2,1,0:T(8,128)(2,1)}, u32[]{:S(2)}, u32[]{:S(2)}) collective-permute-start(bf16[16,64,576]{2,1,0:T(8,128)(2,1)} %all-to-all-done.2), channel_id=1, source_target_pairs={{0,16},{16,0},{1,17},{17,1},{2,18},{18,2},{3,19},{19,3},{4,20},{20... | collective-permute-start | bytes 3538952 | tf_op jit(solution)/shard_map/ppermute | solution.py:146
  80.5 6.5 %copy-start.1 = (bf16[8,512,128]{2,1,0:T(8,128)(2,1)S(1)}, bf16[8,512,128]{2,1,0:T(8,128)(2,1)}, u32[]{:S(2)}) copy-start(bf16[8,512,128]{2,1,0:T(8,128)(2,1)} %uv_ref.1) | copy-start | bytes 3145732

commit v2 on v0

v2 whole, which is shorter than its diff:
```python
import functools

import jax
import jax.numpy as jnp
from jax import lax
from jax.experimental import pallas as pl
from jax.experimental.pallas import tpu as pltpu
from jax.sharding import Mesh, PartitionSpec as P

softmax_scale = 192.0 ** (-0.5)
lowest_score = -1e30
log2_scale = softmax_scale * 1.4426950408889634

axis_names = ("zh", "y", "c", "x", "zl")
axis_sizes = (4, 4, 2, 4, 4)
group_axes = ("zh", "y", "c")
head_axes = ("x", "zl")


def from_high(high, piece):
    place = lax.axis_index("zh")
    up, down, across = (high + 1) % 4, (high + 3) % 4, (high + 2) % 4
    above = lax.ppermute(piece, "zh", [(high, up)])
    below = lax.ppermute(piece, "zh", [(high, down)])
    beyond = lax.ppermute(above, "zh", [(up, across)])
    result = jnp.where(place == up, above, piece)
    result = jnp.where(place == down, below, result)
    return jnp.where(place == across, beyond, result)


def gathered(value, axes, count):
    tiled = jnp.broadcast_to(value[None], (count,) + value.shape)
    return lax.all_to_all(tiled, axes, 0, 0, tiled=True)


def scores_of(query, keys):
    return lax.dot_general(
        query, keys, (((1,), (1,)), ((), ())), preferred_element_type=jnp.float32
    )


def read_stats(stats_ref, at):
    return stats_ref[at, 0:1], stats_ref[at, 1:2]


def write_stats(stats_ref, at, maxima, sums):
    rows = maxima.shape[0]
    lane = lax.broadcasted_iota(jnp.int32, (rows, stats_ref.shape[1]), 1)
    stats_ref[at, :] = jnp.where(lane == 0, maxima, sums)


def write_places(page_len, piece_rows, table_ref, places_ref):
    shape = (8, places_ref.shape[1])
    lane = lax.broadcasted_iota(jnp.int32, shape, 1)
    offset = lane % piece_rows
    low = lane // piece_rows % 4
    lower = lane // (piece_rows * 4) % 2
    page = lane // (piece_rows * 8) % 2
    slot = (lane // (piece_rows * 16) * 4 + low) * 2 + page
    places = lower * (2 * piece_rows) + offset
    for logical in range(table_ref.shape[0]):
        places += jnp.where(slot == table_ref[logical], logical * page_len, 0)
    core = lax.axis_index("c")
    places_ref[0:8, :] = places + core * piece_rows
    places_ref[8:16, :] = places + (1 - core) * piece_rows


def local_kernel(heads, steps, block, page_len, piece_rows, table_ref, query_ref, own_ref, new_ref,
                 stats_ref, acc_ref, places_ref):
    write_places(page_len, piece_rows, table_ref, places_ref)
    rows = query_ref.shape[0]
    rank_dim = acc_ref.shape[1]
    per_request = heads * steps
    requests = rows // per_request
    own_len = own_ref.shape[0] // requests
    per_block = block // per_request
    row = lax.broadcasted_iota(jnp.int32, (block, per_block * own_len), 0)
    key = lax.broadcasted_iota(jnp.int32, (block, per_block * own_len), 1)
    own_seen = row // per_request == key // own_len
    row = lax.broadcasted_iota(jnp.int32, (block, per_block * steps), 0)
    key = lax.broadcasted_iota(jnp.int32, (block, per_block * steps), 1)
    new_seen = (row // per_request == key // steps) & (
        key % steps <= (row % per_request) // heads
    )
    for number in range(rows // block):
        at = slice(number * block, (number + 1) * block)
        query = query_ref[at, :]
        own = own_ref[number * per_block * own_len : (number + 1) * per_block * own_len, :]
        new = new_ref[number * per_block * steps : (number + 1) * per_block * steps, :]
        own_scores = jnp.where(own_seen, scores_of(query, own), lowest_score)
        new_scores = jnp.where(new_seen, scores_of(query, new), lowest_score)
        maxima = jnp.maximum(
            jnp.max(own_scores, axis=1, keepdims=True), jnp.max(new_scores, axis=1, keepdims=True)
        )
        own_exp = jnp.exp2(own_scores * log2_scale - maxima * log2_scale)
        new_exp = jnp.exp2(new_scores * log2_scale - maxima * log2_scale)
        sums = jnp.sum(own_exp, axis=1, keepdims=True) + jnp.sum(new_exp, axis=1, keepdims=True)
        acc_ref[at, :] = jnp.dot(
            own_exp.astype(jnp.bfloat16), own[:, :rank_dim], preferred_element_type=jnp.float32
        ) + jnp.dot(
            new_exp.astype(jnp.bfloat16), new[:, :rank_dim], preferred_element_type=jnp.float32
        )
        write_stats(stats_ref, at, maxima, sums)


def prompt_kernel(block, rows_per_request, half, rank_dim, finish, lens_ref, route_ref, query_ref,
                  keys_ref, places_ref):
    count = query_ref.shape[0] // block
    key_count = keys_ref.shape[0]
    per_block = block // rows_per_request
    active = route_ref[0] > 0
    places = places_ref[half * 8 : (half + 1) * 8, :]
    scores = scores_of(query_ref[0:block, :], keys_ref[...])
    for number in range(count):
        at = slice(number * block, (number + 1) * block)
        following = None
        if number + 1 < count:
            following = scores_of(
                query_ref[(number + 1) * block : (number + 2) * block, :], keys_ref[...]
            )
        parts = []
        for request in range(per_block):
            seen = places < jnp.where(active, lens_ref[number * per_block + request], 0)
            part = scores[request * rows_per_request : (request + 1) * rows_per_request]
            part = part.reshape(rows_per_request // 8, 8, key_count)
            part = jnp.where(seen[None], part, lowest_score)
            parts.append(part.reshape(rows_per_request, key_count))
        scores = jnp.concatenate(parts, axis=0)
        maxima = jnp.max(scores, axis=1, keepdims=True)
        expons = jnp.exp2(scores * log2_scale - maxima * log2_scale)
        sums = jnp.sum(expons, axis=1, keepdims=True)
        weighted = jnp.dot(
            expons.astype(jnp.bfloat16), keys_ref[:, :rank_dim],
            preferred_element_type=jnp.float32,
        )
        finish(number, at, maxima, sums, weighted)
        scores = following


def first_kernel(block, rows_per_request, lens_ref, route_ref, query_ref, keys_ref, places_ref,
                 stats_ref, acc_ref):

    def keep(number, at, maxima, sums, weighted):
        acc_ref[at, :] = weighted
        write_stats(stats_ref, at, maxima, sums)

    prompt_kernel(
        block, rows_per_request, 0, acc_ref.shape[1], keep, lens_ref, route_ref, query_ref,
        keys_ref, places_ref,
    )


def last_kernel(block, rows_per_request, heads, lens_ref, route_ref, query_ref, keys_ref,
                places_ref, stats_ref, acc_ref, local_stats_ref, local_ref, uv_ref, out_ref,
                latent_ref):
    def divide(number, at, maxima, sums, weighted):
        first_max, first_sums = read_stats(stats_ref, at)
        local_max, local_sums = read_stats(local_stats_ref, at)
        peak = jnp.maximum(jnp.maximum(maxima, first_max), local_max)
        factor = jnp.exp2((maxima - peak) * log2_scale)
        first_factor = jnp.exp2((first_max - peak) * log2_scale)
        local_factor = jnp.exp2((local_max - peak) * log2_scale)
        inverse = 1.0 / (sums * factor + first_sums * first_factor + local_sums * local_factor)
        latent = (
            weighted * (factor * inverse)
            + acc_ref[at, :] * (first_factor * inverse)
            + local_ref[at, :] * (local_factor * inverse)
        )
        latent = latent.astype(jnp.bfloat16).astype(jnp.float32)
        for part in range(latent_ref.shape[0]):
            latent_ref[part, at, :] = latent[:, part * 128 : (part + 1) * 128]

    prompt_kernel(
        block, rows_per_request, 1, acc_ref.shape[1], divide, lens_ref, route_ref, query_ref,
        keys_ref, places_ref,
    )
    requests, steps = out_ref.shape[:2]
    vhead = uv_ref.shape[2]
    for head in range(heads):
        rows = jnp.concatenate(
            [
                latent_ref[part, pl.ds(head, requests * steps, stride=heads), :].astype(jnp.bfloat16)
                for part in range(latent_ref.shape[0])
            ],
            axis=1,
        )
        product = jnp.dot(rows, uv_ref[head], preferred_element_type=jnp.float32)
        out_ref[:, :, head * vhead : (head + 1) * vhead] = product.reshape(
            requests, steps, vhead
        ).astype(jnp.bfloat16)


def body(
    queries, new_latent, own_cache, prompt_pool, uv_weight, owner, route, prompt_len, page_table
):
    requests, num_steps, head_dev, latent = queries.shape
    rank_dim = uv_weight.shape[1]
    vhead_dim = uv_weight.shape[2]
    num_pages = page_table.shape[0]
    own_pages, page_len = prompt_pool.shape[1:3]
    row_count = requests * num_steps * head_dev
    rows_per_request = num_steps * head_dev
    query_rows = queries.reshape(row_count, latent)

    group_ids = jnp.arange(owner.shape[0], dtype=jnp.int32)
    root = jnp.sum(jnp.where(owner == 0, group_ids, 0))
    root_high = root // 8
    root_piece = root % 8

    pieces = prompt_pool.reshape(8, own_pages * page_len // 8, latent)
    pieces = lax.all_to_all(pieces, ("y", "c"), 0, 0, tiled=True)
    piece = lax.dynamic_index_in_dim(pieces, root_piece, 0, keepdims=False)
    piece = lax.switch(root_high, [functools.partial(from_high, high) for high in range(4)], piece)
    run = gathered(piece, "zl", 4)
    half = gathered(run.reshape(-1, latent), ("x", "y"), 16)
    block = 256
    vmem = pl.BlockSpec(memory_space=pltpu.VMEM)
    smem = pl.BlockSpec(memory_space=pltpu.SMEM)
    params = pltpu.CompilerParams(vmem_limit_bytes=12 * 1024 * 1024)
    stats_shape = [
        jax.ShapeDtypeStruct((row_count, 128), jnp.float32),
        jax.ShapeDtypeStruct((row_count, rank_dim), jnp.float32),
    ]
    key_count = num_pages * page_len // 2
    local = pl.pallas_call(
        functools.partial(
            local_kernel, head_dev, num_steps, block, page_len, own_pages * page_len // 8
        ),
        in_specs=[smem] + [vmem] * 3,
        out_specs=[vmem] * 3,
        out_shape=stats_shape + [jax.ShapeDtypeStruct((16, key_count), jnp.int32)],
        compiler_params=params,
        cost_estimate=pl.CostEstimate(
            flops=2 * row_count * block * (latent + rank_dim) * 2,
            bytes_accessed=8 * row_count * rank_dim,
            transcendentals=row_count * block,
        ),
    )
    stats, acc, places = local(
        page_table, query_rows, own_cache.reshape(-1, latent), new_latent.reshape(-1, latent)
    )
    half, stats, acc, places = lax.optimization_barrier((half, stats, acc, places))
    other = lax.ppermute(half, "c", [(0, 1), (1, 0)]).reshape(-1, latent)
    half = half.reshape(-1, latent)
    cost = pl.CostEstimate(
        flops=2 * row_count * key_count * (latent + rank_dim),
        bytes_accessed=2 * (row_count + key_count) * latent + 4 * row_count * rank_dim,
        transcendentals=row_count * key_count,
    )
    wide = pltpu.CompilerParams(vmem_limit_bytes=20 * 1024 * 1024)
    first = pl.pallas_call(
        functools.partial(first_kernel, block, rows_per_request),
        in_specs=[smem, smem] + [vmem] * 3,
        out_specs=[vmem] * 2,
        out_shape=stats_shape,
        compiler_params=wide,
        cost_estimate=cost,
    )
    first_stats, first_acc = first(prompt_len, route, query_rows, half, places)
    last = pl.pallas_call(
        functools.partial(last_kernel, block, rows_per_request, head_dev),
        in_specs=[smem, smem] + [vmem] * 8,
        out_specs=vmem,
        scratch_shapes=[pltpu.VMEM((rank_dim // 128, row_count, 128), jnp.float32)],
        out_shape=jax.ShapeDtypeStruct((requests, num_steps, head_dev * vhead_dim), jnp.bfloat16),
        compiler_params=wide,
        cost_estimate=cost,
    )
    return last(
        prompt_len, route, query_rows, other, places, first_stats, first_acc, stats, acc, uv_weight
    )


def solution(mesh):
    fine = Mesh(mesh.devices.reshape(axis_sizes), axis_names)
    placed = (
        P(group_axes, None, head_axes, None),
        P(group_axes, None, None),
        P(group_axes, None, None),
        P(group_axes, head_axes, None, None),
        P(head_axes, None, None),
        P(),
        P(group_axes),
        P(group_axes),
        P(),
    )
    return jax.shard_map(
        body, mesh=fine, in_specs=placed, out_specs=P(group_axes, None, head_axes), check_vma=False
    )
```

time: 463 us -> 76.7 us (0.17); the launches traced: 454 us -> 76.2 us
  waiting for transfers between devices: 411 us -> 19 us
  starting transfers between devices: 0.04 us -> 25.8 us
  Pallas kernels: 0 us -> 14.3 us
  matrix products: 13.2 us -> 0 us
  between operations: 14.8 us -> 3.37 us
  blocking collectives: 0 us -> 7.36 us
  other arithmetic: 6.69 us -> 1.3 us
    psum x1 -> x0, waiting for transfers between devices: 335 us -> none  [from_root(): return lax.psum(jnp.where(mine, value, jnp.zeros_like(value)), axis)]
    all_gather x1 -> x0, waiting for transfers between devices: 76.9 us -> none  [body(): arrived = lax.all_gather(shard, 'head', axis=1, tiled=True)]
    all_to_all x0 -> x2, starting transfers between devices: none -> 15.5 us  [the longest x1 10.2 us: body(): pieces = lax.all_to_all(pieces, ('y', 'c'), 0, 0, tiled=True)]
    pallas_call x0 -> x3, Pallas kernels: none -> 14.3 us  [the longest x1 6.43 us: body(): last(prompt_len, route, query_rows, other, places, first_stats, first_acc...]
    dot_general x5 -> x0, matrix products: 13.2 us -> none  [the longest x1 6.73 us: block_stats(): lax.dot_general(query_rows, key_rows, (((1,), (1,)), ((), ())), preferred...]
    all_to_all x0 -> x2, waiting for transfers between devices: none -> 11.3 us  [the longest x1 9.65 us: gathered(): return lax.all_to_all(tiled, axes, 0, 0, tiled=True)]
    ppermute x0 -> x4, starting transfers between devices: none -> 10.3 us  [the longest x1 7.11 us: body(): other = lax.ppermute(half, 'c', [(0, 1), (1, 0)]).reshape(-1, latent)]
    ppermute x0 -> x4, waiting for transfers between devices: none -> 7.69 us  [the longest x1 6.81 us: from_high(): above = lax.ppermute(piece, 'zh', [(high, up)])]
  transfers between devices with their start and end apart: 2 -> 6, of which waited for: 2 -> 4; matrix products, arithmetic and copies ran while one was open for 2% -> 3% of each run, Pallas kernels for 0% -> 10%
where the time goes in v2:
time: 76.7 us; the launch traced here: 76.2 us
  starting transfers between devices  25.8 us (34%)
  waiting for transfers between devices  19 us (25%)
  Pallas kernels  14.3 us (19%)
  blocking collectives  7.36 us (10%)
  local copies, waits for them, and re-layouts  5.01 us (7%)
  between operations  3.37 us (4%)
  other arithmetic  1.3 us (2%)
    all_to_all x1, starting transfers between devices, body(): pieces = lax.all_to_all(pieces, ('y', 'c'), 0, 0, tiled=True)  10.2 us
    all_to_all x1, waiting for transfers between devices, gathered(): return lax.all_to_all(tiled, axes, 0, 0, tiled=True)  9.65 us
    all_to_all x1, blocking collectives, gathered(): return lax.all_to_all(tiled, axes, 0, 0, tiled=True)  7.36 us
    ppermute x1, starting transfers between devices, body(): other = lax.ppermute(half, 'c', [(0, 1), (1, 0)]).reshape(-1, latent)  7.11 us
    ppermute x1, waiting for transfers between devices, from_high(): above = lax.ppermute(piece, 'zh', [(high, up)])  6.81 us
    pallas_call x1, Pallas kernels, body(): last(prompt_len, route, query_rows, other, places, first_stats, first_acc...  6.43 us
    all_to_all x1, starting transfers between devices, gathered(): return lax.all_to_all(tiled, axes, 0, 0, tiled=True)  5.31 us
    pallas_call x1, Pallas kernels, body(): first_stats, first_acc = first(prompt_len, route, query_rows, half, places)  4.78 us
  transfers between devices with their start and end apart: 6, of which 4 were waited for; matrix products, arithmetic and copies ran while one was open for 3% of the time, Pallas kernels for 10%

profile of v2, /device:TPU:1, one launch (start us, length us, event | category | flops | bytes accessed | tf_op | source)
XLA Modules:
  0.0 76.2 jit_solution(15138001862594634771)
XLA Ops:
  0.0 10.2 %all-to-all-start = ((bf16[8,16,576]{2,1,0:T(8,128)(2,1)}), bf16[8,16,576]{2,1,0:T(8,128)(2,1)S(1)}, u32[]{:S(2)}, u32[]{:S(2)}) async-start(bf16[8,16,576]{2,1,0:T(8,128)(2,1)} %bitcast.14), calls=%async_computation | async-start | bytes 327680 | tf_op jit(solution)/shard_map/all_to_all | solution.py:211
  10.2 1.3 %fusion = s32[]{:T(128)} fusion(s32[32]{0:T(128)} %param.18), kind=kLoop, calls=%fused_computation.6 | loop fusion | flops 95 | bytes 132 | tf_op jit(solution)/shard_map/reduce_sum | solution.py:206
  14.1 1.7 %all-to-all-done = bf16[8,16,576]{2,1,0:T(8,128)(2,1)S(1)} async-done(((bf16[8,16,576]{2,1,0:T(8,128)(2,1)}), bf16[8,16,576]{2,1,0:T(8,128)(2,1)S(1)}, u32[]{:S(2)}, u32[]{:S(2)}) %all-to-all-start) | async-done | bytes 147488 | tf_op jit(solution)/shard_map/all_to_all | solution.py:211
  15.8 11.0 %conditional.1 = (bf16[16,576]{1,0:T(8,128)(2,1)S(1)}) conditional(s32[]{:T(128)} %clamp.3, bf16[16,576]{1,0:T(8,128)(2,1)S(1)} %dynamic-slice_bitcast_fusion, bf16[16,576]{1,0:T(8,128)(2,1)S(1)} %dynamic-slice_bitcast_fusion, bf16[16,576]{1,0:T(8,128)(2,1)S(1)} %dynamic-slice_bitcast_fusion, ...), branch_computations={%region_1.2_spmd, %region_2.3_spmd, %region_3.4_spmd, %region_4.5_... | conditional | flops 27654 | bytes 313534 | solution.py:213
  15.8 1.3 %collective-permute-start.9 = (bf16[16,576]{1,0:T(8,128)(2,1)S(1)}, bf16[16,576]{1,0:T(8,128)(2,1)S(1)}, u32[]{:S(2)}, u32[]{:S(2)}) collective-permute-start(bf16[16,576]{1,0:T(8,128)(2,1)S(1)} %param.3), channel_id=1, source_target_pairs={{384,0},{385,1},{386,2},{387,3},{388,4},{389,5},{390,6},{391,7},{3... | collective-permute-start | bytes 55304 | tf_op jit(solution)/shard_map/cond/branch_3_fun/ppermute | solution.py:23
  17.1 0.7 collective-permute-start.11
  17.7 6.8 %collective-permute-done.9 = bf16[16,576]{1,0:T(8,128)(2,1)S(1)} collective-permute-done((bf16[16,576]{1,0:T(8,128)(2,1)S(1)}, bf16[16,576]{1,0:T(8,128)(2,1)S(1)}, u32[]{:S(2)}, u32[]{:S(2)}) %collective-permute-start.9) | collective-permute-done | bytes 18464 | tf_op jit(solution)/shard_map/cond/branch_3_fun/ppermute | solution.py:23
  24.5 1.3 %collective-permute-start.10 = (bf16[16,576]{1,0:T(8,128)(2,1)S(1)}, bf16[16,576]{1,0:T(8,128)(2,1)S(1)}, u32[]{:S(2)}, u32[]{:S(2)}) collective-permute-start(bf16[16,576]{1,0:T(8,128)(2,1)S(1)} %collective-permute-done.9), channel_id=1, source_target_pairs={{0,128},{1,129},{2,130},{3,131},{4,132},{5,133},{6,134},{7,135},{8... | collective-permute-start | bytes 55304 | tf_op jit(solution)/shard_map/cond/branch_3_fun/ppermute | solution.py:25
  25.8 0.0 collective-permute-done.11
  25.8 0.9 %collective-permute-done.10 = bf16[16,576]{1,0:T(8,128)(2,1)S(1)} collective-permute-done((bf16[16,576]{1,0:T(8,128)(2,1)S(1)}, bf16[16,576]{1,0:T(8,128)(2,1)S(1)}, u32[]{:S(2)}, u32[]{:S(2)}) %collective-permute-start.10) | collective-permute-done | bytes 18464 | tf_op jit(solution)/shard_map/cond/branch_3_fun/ppermute | solution.py:25
  26.7 7.4 %all_to_all.15 = bf16[4,16,576]{2,1,0:T(8,128)(2,1)S(1)} all-to-all(bf16[4,16,576]{2,1,0:T(8,128)(2,1)S(1)} %broadcast_in_dim.8), channel_id=1, replica_groups=mesh['zh'=4,'y'=4,'c'=2,'x'=4,'zl'=4] {'zl'}, dimensions={0} | all-to-all | bytes 147456 | tf_op jit(solution)/shard_map/all_to_all | solution.py:33
  34.1 1.2 %broadcast_in_dim.17 = bf16[16,64,576]{2,1,0:T(8,128)(2,1)} broadcast(bf16[64,576]{1,0:T(8,128)(2,1)S(1)} %bitcast.13), dimensions={1,2} | broadcast | bytes 1253376 | tf_op jit(solution)/shard_map/broadcast_in_dim | solution.py:32
  35.3 5.3 %all-to-all-start.2 = ((bf16[16,64,576]{2,1,0:T(8,128)(2,1)}), bf16[16,64,576]{2,1,0:T(8,128)(2,1)}, u32[]{:S(2)}, u32[]{:S(2)}) async-start(bf16[16,64,576]{2,1,0:T(8,128)(2,1)} %broadcast_in_dim.17), calls=%async_computation.2 | async-start | bytes 2621440 | tf_op jit(solution)/shard_map/all_to_all | solution.py:33
  40.6 0.7 reshape.23.new_ref
  41.4 0.9 %copy-done.4 = bf16[128,576]{1,0:T(8,128)(2,1)S(1)} copy-done((bf16[128,576]{1,0:T(8,128)(2,1)S(1)}, bf16[128,576]{1,0:T(8,128)(2,1)}, u32[]{:S(2)}) %copy-start.4) | copy-done | bytes 147480
  42.3 1.3 %copy-done.6 = bf16[32,32,576]{2,1,0:T(8,128)(2,1)S(1)} copy-done((bf16[32,32,576]{2,1,0:T(8,128)(2,1)S(1)}, bf16[32,32,576]{2,1,0:T(8,128)(2,1)}, u32[]{:S(2)}) %copy-start.6) | copy-done | bytes 1179672
  43.6 3.1 %shard_map.91 = (f32[1024,128]{1,0:T(8,128)S(1)}, f32[1024,512]{1,0:T(8,128)S(1)}, s32[16,1024]{1,0:T(8,128)S(1)}) custom-call(s32[32]{0:T(128)S(1)} %copy-done.7, bf16[1024,576]{1,0:T(8,128)(2,1)S(1)} %bitcast.8, bf16[1024,576]{1,0:T(8,128)(2,1)S(1)} %bitcast.12, bf16[128,576]{1,0:T(8,128)(2,1)S(1)} %copy-done.4), custom_call_target="tpu_custom_call" | custom-call | flops 1140850688 | bytes 4194304 | tf_op jit(solution)/shard_map/pallas_call | solution.py:239
  46.7 0.8 %copy-done.2 = f32[1024,128]{1,0:T(8,128)} copy-done((f32[1024,128]{1,0:T(8,128)}, f32[1024,128]{1,0:T(8,128)S(1)}, u32[]{:S(2)}) %copy-start.2) | copy-done | bytes 524312
  47.5 9.6 %all-to-all-done.2 = bf16[16,64,576]{2,1,0:T(8,128)(2,1)} async-done(((bf16[16,64,576]{2,1,0:T(8,128)(2,1)}), bf16[16,64,576]{2,1,0:T(8,128)(2,1)}, u32[]{:S(2)}, u32[]{:S(2)}) %all-to-all-start.2) | async-done | bytes 1179680 | tf_op jit(solution)/shard_map/all_to_all | solution.py:33
  57.2 7.1 %collective-permute-start.12 = (bf16[16,64,576]{2,1,0:T(8,128)(2,1)}, bf16[16,64,576]{2,1,0:T(8,128)(2,1)S(1)}, u32[]{:S(2)}, u32[]{:S(2)}) collective-permute-start(bf16[16,64,576]{2,1,0:T(8,128)(2,1)} %all-to-all-done.2), channel_id=1, source_target_pairs={{0,16},{16,0},{1,17},{17,1},{2,18},{18,2},{3,19},{19,3},{4,20},{20... | collective-permute-start | bytes 3538952 | tf_op jit(solution)/shard_map/ppermute | solution.py:243
  64.9 0.0 copy-start.1
  65.0 4.8 %shard_map.92 = (f32[1024,128]{1,0:T(8,128)S(1)}, f32[1024,512]{1,0:T(8,128)S(1)}) custom-call(s32[32]{0:T(128)S(1)} %copy-done.5, s32[1]{0:T(128)S(6)} %copy.14.route_ref, bf16[1024,576]{1,0:T(8,128)(2,1)S(1)} %bitcast.9, bf16[1024,576]{1,0:T(8,128)(2,1)} %bitcast.6.keys_ref, s32[16,1024]{1,0:T(8,128)S(1)} %get-tuple-element.27.places_ref), custom_call_target="tpu_custom_call" | custom-call | flops 2281701376 | bytes 4456448 | tf_op jit(solution)/shard_map/pallas_call | solution.py:259
  69.8 0.0 collective-permute-done.12
  69.8 6.4 %shard_map.93 = bf16[32,4,1024]{2,1,0:T(4,128)(2,1)} custom-call(s32[32]{0:T(128)S(1)} %copy-done.5, s32[1]{0:T(128)S(6)} %copy.14.route_ref, bf16[1024,576]{1,0:T(8,128)(2,1)S(1)} %bitcast.10, bf16[1024,576]{1,0:T(8,128)(2,1)S(1)} %bitcast.11, s32[16,1024]{1,0:T(8,128)S(1)} %get-tuple-element.27.places_ref, f32[1024,128]{1,0:T(8,128)S(1)} %get-tuple-element.28.stats_ref, ...), custom_call_target="tpu_custom_call" | custom-call | flops 2281701376 | bytes 4456448 | tf_op jit(solution)/shard_map/pallas_call | solution.py:269
  (17 shorter events, 0.1 us)
Async XLA Ops:
  0.0 15.8 %all-to-all-start = ((bf16[8,16,576]{2,1,0:T(8,128)(2,1)}), bf16[8,16,576]{2,1,0:T(8,128)(2,1)S(1)}, u32[]{:S(2)}, u32[]{:S(2)}) async-start(bf16[8,16,576]{2,1,0:T(8,128)(2,1)} %bitcast.14), calls=%async_computation | async-start | bytes 327680 | tf_op jit(solution)/shard_map/all_to_all | solution.py:211
  15.8 8.8 %collective-permute-start.9 = (bf16[16,576]{1,0:T(8,128)(2,1)S(1)}, bf16[16,576]{1,0:T(8,128)(2,1)S(1)}, u32[]{:S(2)}, u32[]{:S(2)}) collective-permute-start(bf16[16,576]{1,0:T(8,128)(2,1)S(1)} %param.3), channel_id=1, source_target_pairs={{384,0},{385,1},{386,2},{387,3},{388,4},{389,5},{390,6},{391,7},{3... | collective-permute-start | bytes 55304 | tf_op jit(solution)/shard_map/cond/branch_3_fun/ppermute | solution.py:23
  17.1 8.8 %collective-permute-start.11 = (bf16[16,576]{1,0:T(8,128)(2,1)S(1)}, bf16[16,576]{1,0:T(8,128)(2,1)S(1)}, u32[]{:S(2)}, u32[]{:S(2)}) collective-permute-start(bf16[16,576]{1,0:T(8,128)(2,1)S(1)} %param.3), channel_id=1, source_target_pairs={{384,256},{385,257},{386,258},{387,259},{388,260},{389,261},{390,2... | collective-permute-start | bytes 55304 | tf_op jit(solution)/shard_map/cond/branch_3_fun/ppermute | solution.py:24
  24.5 2.2 %collective-permute-start.10 = (bf16[16,576]{1,0:T(8,128)(2,1)S(1)}, bf16[16,576]{1,0:T(8,128)(2,1)S(1)}, u32[]{:S(2)}, u32[]{:S(2)}) collective-permute-start(bf16[16,576]{1,0:T(8,128)(2,1)S(1)} %collective-permute-done.9), channel_id=1, source_target_pairs={{0,128},{1,129},{2,130},{3,131},{4,132},{5,133},{6,134},{7,135},{8... | collective-permute-start | bytes 55304 | tf_op jit(solution)/shard_map/cond/branch_3_fun/ppermute | solution.py:25
  35.3 5.3 %copy-start.8 = (bf16[32,4,576]{2,1,0:T(4,128)(2,1)S(1)}, bf16[32,4,576]{2,1,0:T(4,128)(2,1)}, u32[]{:S(2)}) copy-start(bf16[32,4,576]{2,1,0:T(4,128)(2,1)} %param.14) | copy-start | bytes 442372
  35.3 6.1 %copy-start = (bf16[32,4,8,576]{3,2,1,0:T(8,128)(2,1)S(1)}, bf16[32,4,8,576]{3,2,1,0:T(8,128)(2,1)}, u32[]{:S(2)}) copy-start(bf16[32,4,8,576]{3,2,1,0:T(8,128)(2,1)} %param.13) | copy-start | bytes 3538948
  35.3 6.1 %copy-start.7 = (s32[32]{0:T(128)S(1)}, s32[32]{0:T(128)}, u32[]{:S(2)}) copy-start(s32[32]{0:T(128)} %table_ref.1) | copy-start | bytes 388
  35.3 21.9 %all-to-all-start.2 = ((bf16[16,64,576]{2,1,0:T(8,128)(2,1)}), bf16[16,64,576]{2,1,0:T(8,128)(2,1)}, u32[]{:S(2)}, u32[]{:S(2)}) async-start(bf16[16,64,576]{2,1,0:T(8,128)(2,1)} %broadcast_in_dim.17), calls=%async_computation.2 | async-start | bytes 2621440 | tf_op jit(solution)/shard_map/all_to_all | solution.py:33
  41.4 0.9 %copy-start.4 = (bf16[128,576]{1,0:T(8,128)(2,1)S(1)}, bf16[128,576]{1,0:T(8,128)(2,1)}, u32[]{:S(2)}) copy-start(bf16[128,576]{1,0:T(8,128)(2,1)} %reshape.23.new_ref) | copy-start | bytes 442372
  42.3 1.3 %copy-start.6 = (bf16[32,32,576]{2,1,0:T(8,128)(2,1)S(1)}, bf16[32,32,576]{2,1,0:T(8,128)(2,1)}, u32[]{:S(2)}) copy-start(bf16[32,32,576]{2,1,0:T(8,128)(2,1)} %param.15) | copy-start | bytes 3538948
  43.6 21.3 %copy-start.5 = (s32[32]{0:T(128)S(1)}, s32[32]{0:T(128)}, u32[]{:S(2)}) copy-start(s32[32]{0:T(128)} %lens_ref.3) | copy-start | bytes 388
  46.7 0.8 %copy-start.2 = (f32[1024,128]{1,0:T(8,128)}, f32[1024,128]{1,0:T(8,128)S(1)}, u32[]{:S(2)}) copy-start(f32[1024,128]{1,0:T(8,128)S(1)} %get-tuple-element.30.local_stats_ref) | copy-start | bytes 1572868
  57.2 12.6 %collective-permute-start.12 = (bf16[16,64,576]{2,1,0:T(8,128)(2,1)}, bf16[16,64,576]{2,1,0:T(8,128)(2,1)S(1)}, u32[]{:S(2)}, u32[]{:S(2)}) collective-permute-start(bf16[16,64,576]{2,1,0:T(8,128)(2,1)} %all-to-all-done.2), channel_id=1, source_target_pairs={{0,16},{16,0},{1,17},{17,1},{2,18},{18,2},{3,19},{19,3},{4,20},{20... | collective-permute-start | bytes 3538952 | tf_op jit(solution)/shard_map/ppermute | solution.py:243
  64.9 4.8 %copy-start.1 = (bf16[8,512,128]{2,1,0:T(8,128)(2,1)S(1)}, bf16[8,512,128]{2,1,0:T(8,128)(2,1)}, u32[]{:S(2)}) copy-start(bf16[8,512,128]{2,1,0:T(8,128)(2,1)} %uv_ref.1) | copy-start | bytes 3145732
  65.0 4.8 %copy-start.3 = (f32[1024,128]{1,0:T(8,128)S(1)}, f32[1024,128]{1,0:T(8,128)}, u32[]{:S(2)}) copy-start(f32[1024,128]{1,0:T(8,128)} %copy-done.2) | copy-start | bytes 1572868

commit v3 on v2

--- a/solution.py
+++ b/solution.py
@@ -52,12 +52,11 @@
 def write_places(page_len, piece_rows, table_ref, places_ref):
     shape = (8, places_ref.shape[1])
     lane = lax.broadcasted_iota(jnp.int32, shape, 1)
-    offset = lane % piece_rows
     low = lane // piece_rows % 4
     lower = lane // (piece_rows * 4) % 2
     page = lane // (piece_rows * 8) % 2
     slot = (lane // (piece_rows * 16) * 4 + low) * 2 + page
-    places = lower * (2 * piece_rows) + offset
+    places = lower * (2 * piece_rows) + lane % piece_rows
     for logical in range(table_ref.shape[0]):
         places += jnp.where(slot == table_ref[logical], logical * page_len, 0)
     core = lax.axis_index("c")
@@ -70,23 +69,21 @@
     write_places(page_len, piece_rows, table_ref, places_ref)
     rows = query_ref.shape[0]
     rank_dim = acc_ref.shape[1]
-    per_request = heads * steps
-    requests = rows // per_request
+    requests = rows // (heads * steps)
     own_len = own_ref.shape[0] // requests
-    per_block = block // per_request
-    row = lax.broadcasted_iota(jnp.int32, (block, per_block * own_len), 0)
+    tokens = block // heads
+    per_block = tokens // steps
+    row = lax.broadcasted_iota(jnp.int32, (block, per_block * own_len), 0) % tokens
     key = lax.broadcasted_iota(jnp.int32, (block, per_block * own_len), 1)
-    own_seen = row // per_request == key // own_len
-    row = lax.broadcasted_iota(jnp.int32, (block, per_block * steps), 0)
-    key = lax.broadcasted_iota(jnp.int32, (block, per_block * steps), 1)
-    new_seen = (row // per_request == key // steps) & (
-        key % steps <= (row % per_request) // heads
-    )
+    own_seen = row // steps == key // own_len
+    row = lax.broadcasted_iota(jnp.int32, (block, tokens), 0) % tokens
+    key = lax.broadcasted_iota(jnp.int32, (block, tokens), 1)
+    new_seen = (row // steps == key // steps) & (key <= row)
     for number in range(rows // block):
         at = slice(number * block, (number + 1) * block)
         query = query_ref[at, :]
         own = own_ref[number * per_block * own_len : (number + 1) * per_block * own_len, :]
-        new = new_ref[number * per_block * steps : (number + 1) * per_block * steps, :]
+        new = new_ref[number * tokens : (number + 1) * tokens, :]
         own_scores = jnp.where(own_seen, scores_of(query, own), lowest_score)
         new_scores = jnp.where(new_seen, scores_of(query, new), lowest_score)
         maxima = jnp.maximum(
@@ -103,13 +100,13 @@
         write_stats(stats_ref, at, maxima, sums)
 
 
-def prompt_kernel(block, rows_per_request, half, rank_dim, finish, lens_ref, route_ref, query_ref,
+def prompt_kernel(block, heads, steps, half, rank_dim, finish, lens_ref, query_ref,
                   keys_ref, places_ref):
     count = query_ref.shape[0] // block
+    tokens = block // heads
     key_count = keys_ref.shape[0]
-    per_block = block // rows_per_request
-    active = route_ref[0] > 0
     places = places_ref[half * 8 : (half + 1) * 8, :]
+    sublane = lax.broadcasted_iota(jnp.int32, places.shape, 0)
     scores = scores_of(query_ref[0:block, :], keys_ref[...])
     for number in range(count):
         at = slice(number * block, (number + 1) * block)
@@ -118,14 +115,13 @@
             following = scores_of(
                 query_ref[(number + 1) * block : (number + 2) * block, :], keys_ref[...]
             )
+        scores = scores.reshape(heads, tokens // 8, 8, key_count)
         parts = []
-        for request in range(per_block):
-            seen = places < jnp.where(active, lens_ref[number * per_block + request], 0)
-            part = scores[request * rows_per_request : (request + 1) * rows_per_request]
-            part = part.reshape(rows_per_request // 8, 8, key_count)
-            part = jnp.where(seen[None], part, lowest_score)
-            parts.append(part.reshape(rows_per_request, key_count))
-        scores = jnp.concatenate(parts, axis=0)
+        for pair in range(tokens // 8):
+            request = (number * tokens + pair * 8) // steps
+            limit = jnp.where(sublane < steps, lens_ref[request], lens_ref[request + 1])
+            parts.append(jnp.where((places < limit)[None], scores[:, pair], lowest_score))
+        scores = jnp.stack(parts, axis=1).reshape(block, key_count)
         maxima = jnp.max(scores, axis=1, keepdims=True)
         expons = jnp.exp2(scores * log2_scale - maxima * log2_scale)
         sums = jnp.sum(expons, axis=1, keepdims=True)
@@ -137,22 +133,23 @@
         scores = following
 
 
-def first_kernel(block, rows_per_request, lens_ref, route_ref, query_ref, keys_ref, places_ref,
+def first_kernel(block, heads, steps, lens_ref, query_ref, keys_ref, places_ref,
                  stats_ref, acc_ref):
-
     def keep(number, at, maxima, sums, weighted):
         acc_ref[at, :] = weighted
         write_stats(stats_ref, at, maxima, sums)
 
     prompt_kernel(
-        block, rows_per_request, 0, acc_ref.shape[1], keep, lens_ref, route_ref, query_ref,
+        block, heads, steps, 0, acc_ref.shape[1], keep, lens_ref, query_ref,
         keys_ref, places_ref,
     )
 
 
-def last_kernel(block, rows_per_request, heads, lens_ref, route_ref, query_ref, keys_ref,
-                places_ref, stats_ref, acc_ref, local_stats_ref, local_ref, uv_ref, out_ref,
-                latent_ref):
+def last_kernel(block, heads, lens_ref, query_ref, keys_ref, places_ref,
+                stats_ref, acc_ref, local_stats_ref, local_ref, uv_ref, out_ref, latent_ref):
+    requests, steps = out_ref.shape[:2]
+    tokens = block // heads
+
     def divide(number, at, maxima, sums, weighted):
         first_max, first_sums = read_stats(stats_ref, at)
         local_max, local_sums = read_stats(local_stats_ref, at)
@@ -165,26 +162,19 @@
             weighted * (factor * inverse)
             + acc_ref[at, :] * (first_factor * inverse)
             + local_ref[at, :] * (local_factor * inverse)
-        )
-        latent = latent.astype(jnp.bfloat16).astype(jnp.float32)
-        for part in range(latent_ref.shape[0]):
-            latent_ref[part, at, :] = latent[:, part * 128 : (part + 1) * 128]
+        ).astype(jnp.bfloat16)
+        for head in range(heads):
+            latent_ref[head, number * tokens : (number + 1) * tokens, :] = latent[
+                head * tokens : (head + 1) * tokens
+            ]
 
     prompt_kernel(
-        block, rows_per_request, 1, acc_ref.shape[1], divide, lens_ref, route_ref, query_ref,
+        block, heads, steps, 1, acc_ref.shape[1], divide, lens_ref, query_ref,
         keys_ref, places_ref,
     )
-    requests, steps = out_ref.shape[:2]
     vhead = uv_ref.shape[2]
     for head in range(heads):
-        rows = jnp.concatenate(
-            [
-                latent_ref[part, pl.ds(head, requests * steps, stride=heads), :].astype(jnp.bfloat16)
-                for part in range(latent_ref.shape[0])
-            ],
-            axis=1,
-        )
-        product = jnp.dot(rows, uv_ref[head], preferred_element_type=jnp.float32)
+        product = jnp.dot(latent_ref[head], uv_ref[head], preferred_element_type=jnp.float32)
         out_ref[:, :, head * vhead : (head + 1) * vhead] = product.reshape(
             requests, steps, vhead
         ).astype(jnp.bfloat16)
@@ -199,21 +189,25 @@
     num_pages = page_table.shape[0]
     own_pages, page_len = prompt_pool.shape[1:3]
     row_count = requests * num_steps * head_dev
-    rows_per_request = num_steps * head_dev
-    query_rows = queries.reshape(row_count, latent)
+    block = 256
+    tokens = block // head_dev
+    query_rows = queries.reshape(-1, tokens, head_dev, latent).transpose(0, 2, 1, 3)
+    query_rows = query_rows.reshape(row_count, latent)
 
     group_ids = jnp.arange(owner.shape[0], dtype=jnp.int32)
     root = jnp.sum(jnp.where(owner == 0, group_ids, 0))
-    root_high = root // 8
-    root_piece = root % 8
+    root_high = jnp.right_shift(root, 3)
+    root_piece = jnp.bitwise_and(root, 7)
 
     pieces = prompt_pool.reshape(8, own_pages * page_len // 8, latent)
     pieces = lax.all_to_all(pieces, ("y", "c"), 0, 0, tiled=True)
-    piece = lax.dynamic_index_in_dim(pieces, root_piece, 0, keepdims=False)
+    piece = lax.dynamic_index_in_dim(
+        pieces, root_piece, 0, keepdims=False, allow_negative_indices=False
+    )
     piece = lax.switch(root_high, [functools.partial(from_high, high) for high in range(4)], piece)
-    run = gathered(piece, "zl", 4)
-    half = gathered(run.reshape(-1, latent), ("x", "y"), 16)
-    block = 256
+    run = gathered(piece, "zl", 4).reshape(-1, latent)
+    half = gathered(run, ("x", "y"), 16)
+
     vmem = pl.BlockSpec(memory_space=pltpu.VMEM)
     smem = pl.BlockSpec(memory_space=pltpu.SMEM)
     params = pltpu.CompilerParams(vmem_limit_bytes=12 * 1024 * 1024)
@@ -239,7 +233,8 @@
     stats, acc, places = local(
         page_table, query_rows, own_cache.reshape(-1, latent), new_latent.reshape(-1, latent)
     )
-    half, stats, acc, places = lax.optimization_barrier((half, stats, acc, places))
+    lens = jnp.where(route[0] > 0, prompt_len, 0)
+    half, stats, acc, places, lens = lax.optimization_barrier((half, stats, acc, places, lens))
     other = lax.ppermute(half, "c", [(0, 1), (1, 0)]).reshape(-1, latent)
     half = half.reshape(-1, latent)
     cost = pl.CostEstimate(
@@ -249,25 +244,26 @@
     )
     wide = pltpu.CompilerParams(vmem_limit_bytes=20 * 1024 * 1024)
     first = pl.pallas_call(
-        functools.partial(first_kernel, block, rows_per_request),
-        in_specs=[smem, smem] + [vmem] * 3,
+        functools.partial(first_kernel, block, head_dev, num_steps),
+        in_specs=[smem] + [vmem] * 3,
         out_specs=[vmem] * 2,
         out_shape=stats_shape,
         compiler_params=wide,
         cost_estimate=cost,
     )
-    first_stats, first_acc = first(prompt_len, route, query_rows, half, places)
+    first_stats, first_acc = first(lens, query_rows, half, places)
     last = pl.pallas_call(
-        functools.partial(last_kernel, block, rows_per_request, head_dev),
-        in_specs=[smem, smem] + [vmem] * 8,
+        functools.partial(last_kernel, block, head_dev),
+        in_specs=[smem] + [vmem] * 8,
         out_specs=vmem,
-        scratch_shapes=[pltpu.VMEM((rank_dim // 128, row_count, 128), jnp.float32)],
+        scratch_shapes=[pltpu.VMEM((head_dev, requests * num_steps, rank_dim), jnp.bfloat16)],
         out_shape=jax.ShapeDtypeStruct((requests, num_steps, head_dev * vhead_dim), jnp.bfloat16),
         compiler_params=wide,
         cost_estimate=cost,
     )
     return last(
-        prompt_len, route, query_rows, other, places, first_stats, first_acc, stats, acc, uv_weight
+        lens, query_rows, other, places, first_stats, first_acc, stats, acc,
+        uv_weight,
     )
 
 

time: 76.7 us -> 73.3 us (0.956)
  waiting for transfers between devices: 19 us -> 13.3 us
  starting transfers between devices: 25.8 us -> 31 us
  between operations: 3.37 us -> 2.07 us
  local copies, waits for them, and re-layouts: 5.01 us -> 4.17 us
    ppermute x1, waiting for transfers between devices: 6.81 us -> 0.01 us  [from_high(): above = lax.ppermute(piece, 'zh', [(high, up)])]
    ppermute x1, starting transfers between devices: 0.66 us -> 4.3 us  [from_high(): below = lax.ppermute(piece, 'zh', [(high, down)])]
    ppermute x1, starting transfers between devices: 1.28 us -> 4.59 us  [from_high(): above = lax.ppermute(piece, 'zh', [(high, up)])]
    all_to_all x1, waiting for transfers between devices: 1.69 us -> 3.01 us  [body(): pieces = lax.all_to_all(pieces, ('y', 'c'), 0, 0, tiled=True)]
    unnamed x18, local copies, waits for them, and re-layouts: 3.05 us -> 2.03 us
    ppermute x1, waiting for transfers between devices: 0.87 us -> 0.01 us  [from_high(): beyond = lax.ppermute(above, 'zh', [(up, across)])]
  transfers between devices with their start and end apart: 6 -> 6, of which waited for: 4 -> 3; matrix products, arithmetic and copies ran while one was open for 3% -> 3% of each run, Pallas kernels for 10% -> 11%
where the time goes in v3:
time: 73.3 us; the launch traced here: 72.8 us
  starting transfers between devices  31 us (42%)
  Pallas kernels  13.6 us (19%)
  waiting for transfers between devices  13.3 us (18%)
  blocking collectives  7.36 us (10%)
  local copies, waits for them, and re-layouts  4.17 us (6%)
  between operations  2.07 us (3%)
  other arithmetic  1.31 us (2%)
    all_to_all x1, starting transfers between devices, body(): pieces = lax.all_to_all(pieces, ('y', 'c'), 0, 0, tiled=True)  10.2 us
    all_to_all x1, waiting for transfers between devices, gathered(): return lax.all_to_all(tiled, axes, 0, 0, tiled=True)  10.1 us
    all_to_all x1, blocking collectives, gathered(): return lax.all_to_all(tiled, axes, 0, 0, tiled=True)  7.36 us
    ppermute x1, starting transfers between devices, body(): other = lax.ppermute(half, 'c', [(0, 1), (1, 0)]).reshape(-1, latent)  6.37 us
    pallas_call x1, Pallas kernels, body(): last(lens, query_rows, other, places, first_stats, first_acc, stats, acc,...  5.76 us
    all_to_all x1, starting transfers between devices, gathered(): return lax.all_to_all(tiled, axes, 0, 0, tiled=True)  4.9 us
    pallas_call x1, Pallas kernels, body(): first_stats, first_acc = first(lens, query_rows, half, places)  4.74 us
    ppermute x1, starting transfers between devices, from_high(): above = lax.ppermute(piece, 'zh', [(high, up)])  4.59 us
  transfers between devices with their start and end apart: 6, of which 3 were waited for; matrix products, arithmetic and copies ran while one was open for 3% of the time, Pallas kernels for 11%

profile of v3, /device:TPU:1, one launch (start us, length us, event | category | flops | bytes accessed | tf_op | source)
XLA Modules:
  0.0 72.8 jit_solution(13536438874290521416)
XLA Ops:
  0.0 10.2 %all-to-all-start = ((bf16[8,16,576]{2,1,0:T(8,128)(2,1)}), bf16[8,16,576]{2,1,0:T(8,128)(2,1)S(1)}, u32[]{:S(2)}, u32[]{:S(2)}) async-start(bf16[8,16,576]{2,1,0:T(8,128)(2,1)} %bitcast.19), calls=%async_computation | async-start | bytes 327680 | tf_op jit(solution)/shard_map/all_to_all | solution.py:203
  10.2 1.3 %fusion = s32[]{:T(128)} fusion(s32[32]{0:T(128)} %param.18), kind=kLoop, calls=%fused_computation.7 | loop fusion | flops 95 | bytes 132 | tf_op jit(solution)/shard_map/reduce_sum | solution.py:198
  12.8 3.0 %all-to-all-done = bf16[8,16,576]{2,1,0:T(8,128)(2,1)S(1)} async-done(((bf16[8,16,576]{2,1,0:T(8,128)(2,1)}), bf16[8,16,576]{2,1,0:T(8,128)(2,1)S(1)}, u32[]{:S(2)}, u32[]{:S(2)}) %all-to-all-start) | async-done | bytes 147488 | tf_op jit(solution)/shard_map/all_to_all | solution.py:203
  15.8 9.8 %conditional.1 = (bf16[16,576]{1,0:T(8,128)(2,1)S(1)}) conditional(s32[]{:T(128)} %clamp.3, bf16[16,576]{1,0:T(8,128)(2,1)S(1)} %dynamic-slice_bitcast_fusion, bf16[16,576]{1,0:T(8,128)(2,1)S(1)} %dynamic-slice_bitcast_fusion, bf16[16,576]{1,0:T(8,128)(2,1)S(1)} %dynamic-slice_bitcast_fusion, ...), branch_computations={%region_1.2_spmd, %region_2.3_spmd, %region_3.4_spmd, %region_4.5_... | conditional | flops 27654 | bytes 313534 | solution.py:207
  15.8 4.6 %collective-permute-start = (bf16[16,576]{1,0:T(8,128)(2,1)S(1)}, bf16[16,576]{1,0:T(8,128)(2,1)S(1)}, u32[]{:S(2)}, u32[]{:S(2)}) collective-permute-start(bf16[16,576]{1,0:T(8,128)(2,1)S(1)} %param), channel_id=1, source_target_pairs={{0,128},{1,129},{2,130},{3,131},{4,132},{5,133},{6,134},{7,135},{8... | collective-permute-start | bytes 55304 | tf_op jit(solution)/shard_map/cond/branch_0_fun/ppermute | solution.py:23
  20.4 4.3 %collective-permute-start.2 = (bf16[16,576]{1,0:T(8,128)(2,1)S(1)}, bf16[16,576]{1,0:T(8,128)(2,1)S(1)}, u32[]{:S(2)}, u32[]{:S(2)}) collective-permute-start(bf16[16,576]{1,0:T(8,128)(2,1)S(1)} %param), channel_id=1, source_target_pairs={{0,384},{1,385},{2,386},{3,387},{4,388},{5,389},{6,390},{7,391},{8... | collective-permute-start | bytes 55304 | tf_op jit(solution)/shard_map/cond/branch_0_fun/ppermute | solution.py:24
  24.7 0.0 collective-permute-done
  24.7 0.7 collective-permute-start.1
  25.4 0.2 collective-permute-done.2
  25.6 0.0 collective-permute-done.1
  25.6 7.4 %all_to_all.15 = bf16[4,16,576]{2,1,0:T(8,128)(2,1)S(1)} all-to-all(bf16[4,16,576]{2,1,0:T(8,128)(2,1)S(1)} %broadcast_in_dim.9), channel_id=1, replica_groups=mesh['zh'=4,'y'=4,'c'=2,'x'=4,'zl'=4] {'zl'}, dimensions={0} | all-to-all | bytes 147456 | tf_op jit(solution)/shard_map/all_to_all | solution.py:33
  33.0 1.2 %broadcast_in_dim.19 = bf16[16,64,576]{2,1,0:T(8,128)(2,1)} broadcast(bf16[64,576]{1,0:T(8,128)(2,1)S(1)} %bitcast.18), dimensions={1,2} | broadcast | bytes 1253376 | tf_op jit(solution)/shard_map/broadcast_in_dim | solution.py:32
  34.2 4.9 %all-to-all-start.2 = ((bf16[16,64,576]{2,1,0:T(8,128)(2,1)}), bf16[16,64,576]{2,1,0:T(8,128)(2,1)}, u32[]{:S(2)}, u32[]{:S(2)}) async-start(bf16[16,64,576]{2,1,0:T(8,128)(2,1)} %broadcast_in_dim.19), calls=%async_computation.2 | async-start | bytes 2621440 | tf_op jit(solution)/shard_map/all_to_all | solution.py:33
  39.8 0.7 %reshape.29.new_ref = bf16[128,576]{1,0:T(8,128)(2,1)} reshape(bf16[32,4,576]{2,1,0:T(4,128)(2,1)S(1)} %copy-done.7) | data formatting | bytes 294912 | tf_op jit(solution)/shard_map/reshape | solution.py:234
  40.5 0.2 copy.11
  40.7 0.7 copy-done.3
  41.4 0.5 copy-done.4
  41.9 3.1 %shard_map.91 = (f32[1024,128]{1,0:T(8,128)S(1)}, f32[1024,512]{1,0:T(8,128)S(1)}, s32[16,1024]{1,0:T(8,128)S(1)}) custom-call(s32[32]{0:T(128)S(1)} %copy-done.5, bf16[1024,576]{1,0:T(8,128)(2,1)S(1)} %bitcast.12, bf16[1024,576]{1,0:T(8,128)(2,1)S(1)} %bitcast.16, bf16[128,576]{1,0:T(8,128)(2,1)S(1)} %copy-done.3), custom_call_target="tpu_custom_call" | custom-call | flops 1140850688 | bytes 4194304 | tf_op jit(solution)/shard_map/pallas_call | solution.py:233
  45.0 0.8 %copy-done.1 = f32[1024,128]{1,0:T(8,128)} copy-done((f32[1024,128]{1,0:T(8,128)}, f32[1024,128]{1,0:T(8,128)S(1)}, u32[]{:S(2)}) %copy-start.1) | copy-done | bytes 524312
  45.8 10.1 %all-to-all-done.2 = bf16[16,64,576]{2,1,0:T(8,128)(2,1)} async-done(((bf16[16,64,576]{2,1,0:T(8,128)(2,1)}), bf16[16,64,576]{2,1,0:T(8,128)(2,1)}, u32[]{:S(2)}, u32[]{:S(2)}) %all-to-all-start.2) | async-done | bytes 1179680 | tf_op jit(solution)/shard_map/all_to_all | solution.py:33
  55.9 6.4 %collective-permute-start.12 = (bf16[16,64,576]{2,1,0:T(8,128)(2,1)}, bf16[16,64,576]{2,1,0:T(8,128)(2,1)S(1)}, u32[]{:S(2)}, u32[]{:S(2)}) collective-permute-start(bf16[16,64,576]{2,1,0:T(8,128)(2,1)} %all-to-all-done.2), channel_id=1, source_target_pairs={{0,16},{16,0},{1,17},{17,1},{2,18},{18,2},{3,19},{19,3},{4,20},{20... | collective-permute-start | bytes 3538952 | tf_op jit(solution)/shard_map/ppermute | solution.py:238
  62.3 0.0 copy-start
  62.3 4.7 %shard_map.92 = (f32[1024,128]{1,0:T(8,128)S(1)}, f32[1024,512]{1,0:T(8,128)S(1)}) custom-call(s32[32]{0:T(128)S(1)} %broadcast_select_fusion.lens_ref, bf16[1024,576]{1,0:T(8,128)(2,1)S(1)} %bitcast.13, bf16[1024,576]{1,0:T(8,128)(2,1)} %bitcast.10.keys_ref, s32[16,1024]{1,0:T(8,128)S(1)} %get-tuple-element.29.places_ref), custom_call_target="tpu_custom_call" | custom-call | flops 2281701376 | bytes 4456448 | tf_op jit(solution)/shard_map/pallas_call | solution.py:254
  67.1 5.8 %shard_map.93 = bf16[32,4,1024]{2,1,0:T(4,128)(2,1)} custom-call(s32[32]{0:T(128)S(1)} %broadcast_select_fusion.lens_ref, bf16[1024,576]{1,0:T(8,128)(2,1)S(1)} %bitcast.14, bf16[1024,576]{1,0:T(8,128)(2,1)S(1)} %bitcast.15, s32[16,1024]{1,0:T(8,128)S(1)} %get-tuple-element.29.places_ref, f32[1024,128]{1,0:T(8,128)S(1)} %get-tuple-element.30.stats_ref, ...), custom_call_target="tpu_custom_call" | custom-call | flops 2281701376 | bytes 4456448 | tf_op jit(solution)/shard_map/pallas_call | solution.py:264
  (19 shorter events, 0.1 us)
Async XLA Ops:
  0.0 15.8 %all-to-all-start = ((bf16[8,16,576]{2,1,0:T(8,128)(2,1)}), bf16[8,16,576]{2,1,0:T(8,128)(2,1)S(1)}, u32[]{:S(2)}, u32[]{:S(2)}) async-start(bf16[8,16,576]{2,1,0:T(8,128)(2,1)} %bitcast.19), calls=%async_computation | async-start | bytes 327680 | tf_op jit(solution)/shard_map/all_to_all | solution.py:203
  15.8 8.9 %collective-permute-start = (bf16[16,576]{1,0:T(8,128)(2,1)S(1)}, bf16[16,576]{1,0:T(8,128)(2,1)S(1)}, u32[]{:S(2)}, u32[]{:S(2)}) collective-permute-start(bf16[16,576]{1,0:T(8,128)(2,1)S(1)} %param), channel_id=1, source_target_pairs={{0,128},{1,129},{2,130},{3,131},{4,132},{5,133},{6,134},{7,135},{8... | collective-permute-start | bytes 55304 | tf_op jit(solution)/shard_map/cond/branch_0_fun/ppermute | solution.py:23
  20.4 5.2 %collective-permute-start.2 = (bf16[16,576]{1,0:T(8,128)(2,1)S(1)}, bf16[16,576]{1,0:T(8,128)(2,1)S(1)}, u32[]{:S(2)}, u32[]{:S(2)}) collective-permute-start(bf16[16,576]{1,0:T(8,128)(2,1)S(1)} %param), channel_id=1, source_target_pairs={{0,384},{1,385},{2,386},{3,387},{4,388},{5,389},{6,390},{7,391},{8... | collective-permute-start | bytes 55304 | tf_op jit(solution)/shard_map/cond/branch_0_fun/ppermute | solution.py:24
  24.7 0.9 %collective-permute-start.1 = (bf16[16,576]{1,0:T(8,128)(2,1)S(1)}, bf16[16,576]{1,0:T(8,128)(2,1)S(1)}, u32[]{:S(2)}, u32[]{:S(2)}) collective-permute-start(bf16[16,576]{1,0:T(8,128)(2,1)S(1)} %collective-permute-done), channel_id=1, source_target_pairs={{128,256},{129,257},{130,258},{131,259},{132,260},{133,261},{134,2... | collective-permute-start | bytes 55304 | tf_op jit(solution)/shard_map/cond/branch_0_fun/ppermute | solution.py:25
  34.2 5.6 %copy-start.7 = (bf16[32,4,576]{2,1,0:T(4,128)(2,1)S(1)}, bf16[32,4,576]{2,1,0:T(4,128)(2,1)}, u32[]{:S(2)}) copy-start(bf16[32,4,576]{2,1,0:T(4,128)(2,1)} %param.14) | copy-start | bytes 442372
  34.2 6.3 %copy-start.6 = (bf16[32,4,8,576]{3,2,1,0:T(8,128)(2,1)S(1)}, bf16[32,4,8,576]{3,2,1,0:T(8,128)(2,1)}, u32[]{:S(2)}) copy-start(bf16[32,4,8,576]{3,2,1,0:T(8,128)(2,1)} %param.13) | copy-start | bytes 3538948
  34.2 21.7 %all-to-all-start.2 = ((bf16[16,64,576]{2,1,0:T(8,128)(2,1)}), bf16[16,64,576]{2,1,0:T(8,128)(2,1)}, u32[]{:S(2)}, u32[]{:S(2)}) async-start(bf16[16,64,576]{2,1,0:T(8,128)(2,1)} %broadcast_in_dim.19), calls=%async_computation.2 | async-start | bytes 2621440 | tf_op jit(solution)/shard_map/all_to_all | solution.py:33
  40.5 0.9 %copy-start.3 = (bf16[128,576]{1,0:T(8,128)(2,1)S(1)}, bf16[128,576]{1,0:T(8,128)(2,1)}, u32[]{:S(2)}) copy-start(bf16[128,576]{1,0:T(8,128)(2,1)} %reshape.29.new_ref) | copy-start | bytes 442372
  40.5 1.4 %copy-start.4 = (bf16[32,32,576]{2,1,0:T(8,128)(2,1)S(1)}, bf16[32,32,576]{2,1,0:T(8,128)(2,1)}, u32[]{:S(2)}) copy-start(bf16[32,32,576]{2,1,0:T(8,128)(2,1)} %param.15) | copy-start | bytes 3538948
  40.5 1.4 %copy-start.5 = (s32[32]{0:T(128)S(1)}, s32[32]{0:T(128)}, u32[]{:S(2)}) copy-start(s32[32]{0:T(128)} %table_ref.1) | copy-start | bytes 388
  41.9 3.9 %copy-start.8 = (s32[32]{0:T(128)S(1)}, s32[32]{0:T(128)}, u32[]{:S(2)}) copy-start(s32[32]{0:T(128)} %param.20) | copy-start | bytes 388
  45.0 0.8 %copy-start.1 = (f32[1024,128]{1,0:T(8,128)}, f32[1024,128]{1,0:T(8,128)S(1)}, u32[]{:S(2)}) copy-start(f32[1024,128]{1,0:T(8,128)S(1)} %get-tuple-element.32.local_stats_ref) | copy-start | bytes 1572868
  55.9 11.1 %collective-permute-start.12 = (bf16[16,64,576]{2,1,0:T(8,128)(2,1)}, bf16[16,64,576]{2,1,0:T(8,128)(2,1)S(1)}, u32[]{:S(2)}, u32[]{:S(2)}) collective-permute-start(bf16[16,64,576]{2,1,0:T(8,128)(2,1)} %all-to-all-done.2), channel_id=1, source_target_pairs={{0,16},{16,0},{1,17},{17,1},{2,18},{18,2},{3,19},{19,3},{4,20},{20... | collective-permute-start | bytes 3538952 | tf_op jit(solution)/shard_map/ppermute | solution.py:238
  62.3 4.8 %copy-start = (bf16[8,512,128]{2,1,0:T(8,128)(2,1)S(1)}, bf16[8,512,128]{2,1,0:T(8,128)(2,1)}, u32[]{:S(2)}) copy-start(bf16[8,512,128]{2,1,0:T(8,128)(2,1)} %uv_ref.1) | copy-start | bytes 3145732
  62.3 4.8 %copy-start.2 = (f32[1024,128]{1,0:T(8,128)S(1)}, f32[1024,128]{1,0:T(8,128)}, u32[]{:S(2)}) copy-start(f32[1024,128]{1,0:T(8,128)} %copy-done.1) | copy-start | bytes 1572868

commit v4 on v3

--- a/solution.py
+++ b/solution.py
@@ -21,11 +21,9 @@
     place = lax.axis_index("zh")
     up, down, across = (high + 1) % 4, (high + 3) % 4, (high + 2) % 4
     above = lax.ppermute(piece, "zh", [(high, up)])
-    below = lax.ppermute(piece, "zh", [(high, down)])
-    beyond = lax.ppermute(above, "zh", [(up, across)])
-    result = jnp.where(place == up, above, piece)
-    result = jnp.where(place == down, below, result)
-    return jnp.where(place == across, beyond, result)
+    held = jnp.where(place == up, above, piece)
+    onward = lax.ppermute(held, "zh", [(high, down), (up, across)])
+    return jnp.where((place == down) | (place == across), onward, held)
 
 
 def gathered(value, axes, count):

time: 73.3 us -> 81 us (1.11)
  waiting for transfers between devices: 13.3 us -> 23.7 us
  starting transfers between devices: 31 us -> 25.7 us
  other arithmetic: 1.31 us -> 2.65 us
    ppermute x2 -> x1, waiting for transfers between devices: 0.2 us -> 12.5 us  [from_high(): onward = lax.ppermute(held, 'zh', [(high, down), (up, across)])]
    ppermute x1, starting transfers between devices: 4.59 us -> 0.65 us  [from_high(): above = lax.ppermute(piece, 'zh', [(high, up)])]
    ppermute x2 -> x1, starting transfers between devices: 4.96 us -> 1.28 us  [from_high(): onward = lax.ppermute(held, 'zh', [(high, down), (up, across)])]
    ppermute x1, starting transfers between devices: 6.37 us -> 8.73 us  [body(): other = lax.ppermute(half, 'c', [(0, 1), (1, 0)]).reshape(-1, latent)]
    all_to_all x1, waiting for transfers between devices: 10.1 us -> 8.21 us  [gathered(): return lax.all_to_all(tiled, axes, 0, 0, tiled=True)]
    select_n x1 -> x2, other arithmetic: 0.01 us -> 1.35 us  [the longest x1 0.74 us: from_high(): return jnp.where((place == down) | (place == across), onward, held)]
  transfers between devices with their start and end apart: 6 -> 5, of which waited for: 3 -> 3; matrix products, arithmetic and copies ran while one was open for 3% -> 4% of each run, Pallas kernels for 11% -> 10%
where the time goes in v4:
time: 81 us; the launch traced here: 80.4 us
  starting transfers between devices  25.7 us (32%)
  waiting for transfers between devices  23.7 us (29%)
  Pallas kernels  14 us (17%)
  blocking collectives  7.36 us (9%)
  local copies, waits for them, and re-layouts  4.91 us (6%)
  other arithmetic  2.65 us (3%)
  between operations  2.06 us (3%)
    ppermute x1, waiting for transfers between devices, from_high(): onward = lax.ppermute(held, 'zh', [(high, down), (up, across)])  12.5 us
    all_to_all x1, starting transfers between devices, body(): pieces = lax.all_to_all(pieces, ('y', 'c'), 0, 0, tiled=True)  10.2 us
    ppermute x1, starting transfers between devices, body(): other = lax.ppermute(half, 'c', [(0, 1), (1, 0)]).reshape(-1, latent)  8.73 us
    all_to_all x1, waiting for transfers between devices, gathered(): return lax.all_to_all(tiled, axes, 0, 0, tiled=True)  8.21 us
    all_to_all x1, blocking collectives, gathered(): return lax.all_to_all(tiled, axes, 0, 0, tiled=True)  7.36 us
    pallas_call x1, Pallas kernels, body(): last(lens, query_rows, other, places, first_stats, first_acc, stats, acc,...  6.15 us
    all_to_all x1, starting transfers between devices, gathered(): return lax.all_to_all(tiled, axes, 0, 0, tiled=True)  4.9 us
    pallas_call x1, Pallas kernels, body(): first_stats, first_acc = first(lens, query_rows, half, places)  4.79 us
  transfers between devices with their start and end apart: 5, of which 3 were waited for; matrix products, arithmetic and copies ran while one was open for 4% of the time, Pallas kernels for 10%

profile of v4, /device:TPU:1, one launch (start us, length us, event | category | flops | bytes accessed | tf_op | source)
XLA Modules:
  0.0 80.4 jit_solution(11583240056459701389)
XLA Ops:
  0.0 10.2 %all-to-all-start = ((bf16[8,16,576]{2,1,0:T(8,128)(2,1)}), bf16[8,16,576]{2,1,0:T(8,128)(2,1)S(1)}, u32[]{:S(2)}, u32[]{:S(2)}) async-start(bf16[8,16,576]{2,1,0:T(8,128)(2,1)} %bitcast.19), calls=%async_computation | async-start | bytes 327680 | tf_op jit(solution)/shard_map/all_to_all | solution.py:201
  10.2 1.3 %fusion = s32[]{:T(128)} fusion(s32[32]{0:T(128)} %param.18), kind=kLoop, calls=%fused_computation.8 | loop fusion | flops 95 | bytes 132 | tf_op jit(solution)/shard_map/reduce_sum | solution.py:196
  12.8 3.0 %all-to-all-done = bf16[8,16,576]{2,1,0:T(8,128)(2,1)S(1)} async-done(((bf16[8,16,576]{2,1,0:T(8,128)(2,1)}), bf16[8,16,576]{2,1,0:T(8,128)(2,1)S(1)}, u32[]{:S(2)}, u32[]{:S(2)}) %all-to-all-start) | async-done | bytes 147488 | tf_op jit(solution)/shard_map/all_to_all | solution.py:201
  15.8 15.8 %conditional.1 = (bf16[16,576]{1,0:T(8,128)(2,1)}, bf16[16,576]{1,0:T(8,128)(2,1)}, bf16[16,576]{1,0:T(8,128)(2,1)S(1)}, s32[]{:T(128)}, s32[]{:T(128)}, /*index=5*/s32[]{:T(128)}, s32[]{:T(128)}) conditional(s32[]{:T(128)} %clamp.3, bf16[16,576]{1,0:T(8,128)(2,1)S(1)} %dynamic-slice_bitcast_fusion, ...), branch_computations={%region_1.2_spmd, %region_2.3_spmd, %region_3.4_spmd, %region_4.5_... | conditional | flops 9220 | bytes 239818 | solution.py:205
  15.8 0.7 collective-permute-start.2
  16.4 0.6 broadcast_select_fusion.1
  17.1 1.3 %collective-permute-start.3 = (bf16[16,576]{1,0:T(8,128)(2,1)}, bf16[16,576]{1,0:T(8,128)(2,1)}, u32[]{:S(2)}, u32[]{:S(2)}) collective-permute-start(bf16[16,576]{1,0:T(8,128)(2,1)} %broadcast_select_fusion.1), channel_id=1, source_target_pairs={{128,0},{256,384},{129,1},{257,385},{130,2},{258,386},{131,3},{259... | collective-permute-start | bytes 55304 | tf_op jit(solution)/shard_map/cond/branch_1_fun/ppermute | solution.py:25
  18.3 0.7 copy.46
  19.1 12.5 %collective-permute-done.3 = bf16[16,576]{1,0:T(8,128)(2,1)} collective-permute-done((bf16[16,576]{1,0:T(8,128)(2,1)}, bf16[16,576]{1,0:T(8,128)(2,1)}, u32[]{:S(2)}, u32[]{:S(2)}) %collective-permute-start.3) | collective-permute-done | bytes 18464 | tf_op jit(solution)/shard_map/cond/branch_1_fun/ppermute | solution.py:25
  31.5 0.7 broadcast_select_fusion.4
  32.3 7.4 %all_to_all.15 = bf16[4,16,576]{2,1,0:T(8,128)(2,1)S(1)} all-to-all(bf16[4,16,576]{2,1,0:T(8,128)(2,1)S(1)} %broadcast_in_dim.9), channel_id=1, replica_groups=mesh['zh'=4,'y'=4,'c'=2,'x'=4,'zl'=4] {'zl'}, dimensions={0} | all-to-all | bytes 147456 | tf_op jit(solution)/shard_map/all_to_all | solution.py:31
  39.6 1.2 %broadcast_in_dim.19 = bf16[16,64,576]{2,1,0:T(8,128)(2,1)} broadcast(bf16[64,576]{1,0:T(8,128)(2,1)S(1)} %bitcast.18), dimensions={1,2} | broadcast | bytes 1253376 | tf_op jit(solution)/shard_map/broadcast_in_dim | solution.py:30
  40.9 4.9 %all-to-all-start.2 = ((bf16[16,64,576]{2,1,0:T(8,128)(2,1)}), bf16[16,64,576]{2,1,0:T(8,128)(2,1)}, u32[]{:S(2)}, u32[]{:S(2)}) async-start(bf16[16,64,576]{2,1,0:T(8,128)(2,1)} %broadcast_in_dim.19), calls=%async_computation.2 | async-start | bytes 2621440 | tf_op jit(solution)/shard_map/all_to_all | solution.py:31
  46.4 0.7 reshape.29.new_ref
  47.2 0.2 copy.11
  47.4 0.7 copy-done.3
  48.1 0.5 copy-done.4
  48.6 3.1 %shard_map.91 = (f32[1024,128]{1,0:T(8,128)S(1)}, f32[1024,512]{1,0:T(8,128)S(1)}, s32[16,1024]{1,0:T(8,128)S(1)}) custom-call(s32[32]{0:T(128)S(1)} %copy-done.5, bf16[1024,576]{1,0:T(8,128)(2,1)S(1)} %bitcast.12, bf16[1024,576]{1,0:T(8,128)(2,1)S(1)} %bitcast.16, bf16[128,576]{1,0:T(8,128)(2,1)S(1)} %copy-done.3), custom_call_target="tpu_custom_call" | custom-call | flops 1140850688 | bytes 4194304 | tf_op jit(solution)/shard_map/pallas_call | solution.py:231
  51.7 0.8 copy-done.1
  52.5 8.2 %all-to-all-done.2 = bf16[16,64,576]{2,1,0:T(8,128)(2,1)} async-done(((bf16[16,64,576]{2,1,0:T(8,128)(2,1)}), bf16[16,64,576]{2,1,0:T(8,128)(2,1)}, u32[]{:S(2)}, u32[]{:S(2)}) %all-to-all-start.2) | async-done | bytes 1179680 | tf_op jit(solution)/shard_map/all_to_all | solution.py:31
  60.7 8.7 %collective-permute-start.8 = (bf16[16,64,576]{2,1,0:T(8,128)(2,1)}, bf16[16,64,576]{2,1,0:T(8,128)(2,1)S(1)}, u32[]{:S(2)}, u32[]{:S(2)}) collective-permute-start(bf16[16,64,576]{2,1,0:T(8,128)(2,1)} %all-to-all-done.2), channel_id=1, source_target_pairs={{0,16},{16,0},{1,17},{17,1},{2,18},{18,2},{3,19},{19,3},{4,20},{20... | collective-permute-start | bytes 3538952 | tf_op jit(solution)/shard_map/ppermute | solution.py:236
  69.4 0.0 copy-start
  69.5 4.8 %shard_map.92 = (f32[1024,128]{1,0:T(8,128)S(1)}, f32[1024,512]{1,0:T(8,128)S(1)}) custom-call(s32[32]{0:T(128)S(1)} %broadcast_select_fusion.5.lens_ref, bf16[1024,576]{1,0:T(8,128)(2,1)S(1)} %bitcast.13, bf16[1024,576]{1,0:T(8,128)(2,1)} %bitcast.10.keys_ref, s32[16,1024]{1,0:T(8,128)S(1)} %get-tuple-element.42.places_ref), custom_call_target="tpu_custom_call" | custom-call | flops 2281701376 | bytes 4456448 | tf_op jit(solution)/shard_map/pallas_call | solution.py:252
  74.3 6.2 %shard_map.93 = bf16[32,4,1024]{2,1,0:T(4,128)(2,1)} custom-call(s32[32]{0:T(128)S(1)} %broadcast_select_fusion.5.lens_ref, bf16[1024,576]{1,0:T(8,128)(2,1)S(1)} %bitcast.14, bf16[1024,576]{1,0:T(8,128)(2,1)S(1)} %bitcast.15, s32[16,1024]{1,0:T(8,128)S(1)} %get-tuple-element.42.places_ref, f32[1024,128]{1,0:T(8,128)S(1)} %get-tuple-element.43.stats_ref, ...), custom_call_target="tpu_custom_call" | custom-call | flops 2281701376 | bytes 4456448 | tf_op jit(solution)/shard_map/pallas_call | solution.py:262
  (19 shorter events, 0.0 us)
Async XLA Ops:
  0.0 15.8 %all-to-all-start = ((bf16[8,16,576]{2,1,0:T(8,128)(2,1)}), bf16[8,16,576]{2,1,0:T(8,128)(2,1)S(1)}, u32[]{:S(2)}, u32[]{:S(2)}) async-start(bf16[8,16,576]{2,1,0:T(8,128)(2,1)} %bitcast.19), calls=%async_computation | async-start | bytes 327680 | tf_op jit(solution)/shard_map/all_to_all | solution.py:201
  15.8 0.7 collective-permute-start.2
  17.1 14.5 %collective-permute-start.3 = (bf16[16,576]{1,0:T(8,128)(2,1)}, bf16[16,576]{1,0:T(8,128)(2,1)}, u32[]{:S(2)}, u32[]{:S(2)}) collective-permute-start(bf16[16,576]{1,0:T(8,128)(2,1)} %broadcast_select_fusion.1), channel_id=1, source_target_pairs={{128,0},{256,384},{129,1},{257,385},{130,2},{258,386},{131,3},{259... | collective-permute-start | bytes 55304 | tf_op jit(solution)/shard_map/cond/branch_1_fun/ppermute | solution.py:25
  40.9 5.6 %copy-start.7 = (bf16[32,4,576]{2,1,0:T(4,128)(2,1)S(1)}, bf16[32,4,576]{2,1,0:T(4,128)(2,1)}, u32[]{:S(2)}) copy-start(bf16[32,4,576]{2,1,0:T(4,128)(2,1)} %param.14) | copy-start | bytes 442372
  40.9 6.3 %copy-start.6 = (bf16[32,4,8,576]{3,2,1,0:T(8,128)(2,1)S(1)}, bf16[32,4,8,576]{3,2,1,0:T(8,128)(2,1)}, u32[]{:S(2)}) copy-start(bf16[32,4,8,576]{3,2,1,0:T(8,128)(2,1)} %param.13) | copy-start | bytes 3538948
  40.9 19.8 %all-to-all-start.2 = ((bf16[16,64,576]{2,1,0:T(8,128)(2,1)}), bf16[16,64,576]{2,1,0:T(8,128)(2,1)}, u32[]{:S(2)}, u32[]{:S(2)}) async-start(bf16[16,64,576]{2,1,0:T(8,128)(2,1)} %broadcast_in_dim.19), calls=%async_computation.2 | async-start | bytes 2621440 | tf_op jit(solution)/shard_map/all_to_all | solution.py:31
  47.2 0.9 %copy-start.3 = (bf16[128,576]{1,0:T(8,128)(2,1)S(1)}, bf16[128,576]{1,0:T(8,128)(2,1)}, u32[]{:S(2)}) copy-start(bf16[128,576]{1,0:T(8,128)(2,1)} %reshape.29.new_ref) | copy-start | bytes 442372
  47.2 1.4 %copy-start.4 = (bf16[32,32,576]{2,1,0:T(8,128)(2,1)S(1)}, bf16[32,32,576]{2,1,0:T(8,128)(2,1)}, u32[]{:S(2)}) copy-start(bf16[32,32,576]{2,1,0:T(8,128)(2,1)} %param.15) | copy-start | bytes 3538948
  47.2 1.4 %copy-start.5 = (s32[32]{0:T(128)S(1)}, s32[32]{0:T(128)}, u32[]{:S(2)}) copy-start(s32[32]{0:T(128)} %table_ref.1) | copy-start | bytes 388
  48.6 3.9 %copy-start.8 = (s32[32]{0:T(128)S(1)}, s32[32]{0:T(128)}, u32[]{:S(2)}) copy-start(s32[32]{0:T(128)} %param.20) | copy-start | bytes 388
  51.7 0.8 copy-start.1
  60.7 13.6 %collective-permute-start.8 = (bf16[16,64,576]{2,1,0:T(8,128)(2,1)}, bf16[16,64,576]{2,1,0:T(8,128)(2,1)S(1)}, u32[]{:S(2)}, u32[]{:S(2)}) collective-permute-start(bf16[16,64,576]{2,1,0:T(8,128)(2,1)} %all-to-all-done.2), channel_id=1, source_target_pairs={{0,16},{16,0},{1,17},{17,1},{2,18},{18,2},{3,19},{19,3},{4,20},{20... | collective-permute-start | bytes 3538952 | tf_op jit(solution)/shard_map/ppermute | solution.py:236
  69.4 4.8 %copy-start = (bf16[8,512,128]{2,1,0:T(8,128)(2,1)S(1)}, bf16[8,512,128]{2,1,0:T(8,128)(2,1)}, u32[]{:S(2)}) copy-start(bf16[8,512,128]{2,1,0:T(8,128)(2,1)} %uv_ref.1) | copy-start | bytes 3145732
  69.5 4.8 %copy-start.2 = (f32[1024,128]{1,0:T(8,128)S(1)}, f32[1024,128]{1,0:T(8,128)}, u32[]{:S(2)}) copy-start(f32[1024,128]{1,0:T(8,128)} %copy-done.1) | copy-start | bytes 1572868
